TPU v7x, 128 devices: a whole 4x4x4 slice. The times are simulated.
128 devices in a mesh: gx: 8 (over x_hi, z), af: 16 (over x_lo, y, core).
Axes of the slice: x: 4 (x_hi: 2, x_lo: 2; x = x_hi * 2 + x_lo), y: 4, z: 4, core: 2. Of those that a mesh axis runs over, the one named last changes fastest.
Arguments:
- displace: bfloat16 [32, 20, 36, 128], P('gx'), may hold values from -6 to 6
- weight_in: bfloat16 [3, 3, 3, 128, 512], P(None, None, None, None, 'af'), may hold values from -0.109375 to 0.109375
- weight_out: bfloat16 [3, 3, 3, 512, 128], P(None, None, None, 'af'), may hold values from -0.109375 to 0.109375
- cotangent: bfloat16 [32, 16, 32, 128], P('gx'), may hold values from -6 to 6
Outputs:
- out_field: bfloat16 [32, 16, 32, 128], P('gx')
- field_grad: float32 [32, 20, 36, 128], P('gx')
- inner_grad: float32 [3, 3, 3, 128, 512], P(None, None, None, None, 'af')
- outer_grad: float32 [3, 3, 3, 512, 128], P(None, None, None, 'af')
All inputs are finite; a program needn't handle non-finite values.
Results may differ from a plain program's by a relative error of at most 0.018.
Values may be sent and summed in bfloat16 or wider, within the bound.
A program may use at most 256 MiB of HBM per device.

v0:
```python
import jax
import jax.numpy as jnp
from jax import lax
from jax.experimental import pallas as pl
from jax.experimental.pallas import tpu as pltpu
from jax.sharding import PartitionSpec as P

MESH = pl.DeviceIdType.MESH
BF = jnp.bfloat16
F32 = jnp.float32

SLAB = 4
CY, CZ = 16, 32
PITCH = 48
LANES = 128
MID = 32
TAPS = 9
HY, HALF = 18, 9
FY, FZ = 20, 36
PLANE = FY * FZ
CELLS = CY * CZ
ORDER = (1, 2, 0, 3)

OUT_PIECE = 2 * CELLS
FIELD_PIECE = 1536
AF_ROWS = (OUT_PIECE, OUT_PIECE, FIELD_PIECE, FIELD_PIECE)
AF_BASE = (0, OUT_PIECE, 2 * OUT_PIECE, 2 * OUT_PIECE + FIELD_PIECE)
AF_TOTAL = sum(AF_ROWS)
GRAD = 3 * TAPS * MID
W_ROWS = 1792


def align(value, by=16):
    return pl.multiple_of(value, by)


def kernel(
    disp, cot, win, wout,
    full_ref, grads_ref,
    raw, D, C, H3, P3, W1T, W1, W2T, W2, AI, AO, DF, FS, EXTRA, B, R, WB, WR, QS, QR,
    land_core, land_out, land_field, land_w,
    load_sem, halo_s, halo_r, core_s, core_r, rs_s, rs_r, ag_s, ag_r, ws_s, ws_r, wg_s, wg_r, store_sem,
):
    gx = lax.axis_index("gx")
    af = lax.axis_index("af")
    core = lax.rem(af, 2)
    y = lax.rem(lax.div(af, 2), 4)
    xl = lax.div(af, 8)
    z = lax.rem(gx, 4)
    xh = lax.div(gx, 4)

    order = ((1, 2), (0, 2), (1, 1), (1, 3), (0, 1), (0, 3), (1, 0))
    af_peers, gx_peers = [], []
    for dx, dy in order:
        x2, y2 = lax.rem(xl + dx, 2), lax.rem(y + dy, 4)
        af_peers.append(((gx, (x2 * 4 + y2) * 2 + core), x2 * 4 + y2))
        x2, z2 = lax.rem(xh + dx, 2), lax.rem(z + dy, 4)
        gx_peers.append(((x2 * 4 + z2, af), x2 * 4 + z2))
    other_core = (gx, af + 1 - 2 * core)
    right = (lax.rem(gx + 1, 8), af)
    left = (lax.rem(gx + 7, 8), af)

    loads = [
        pltpu.make_async_copy(disp, raw, load_sem.at[0]),
        pltpu.make_async_copy(cot, C.at[pl.ds(1, SLAB), pl.ds(2, CY)], load_sem.at[1]),
    ]
    for load in loads:
        load.start()
    barrier = pltpu.get_barrier_semaphore()
    peers = [peer for peer, _ in af_peers + gx_peers] + [other_core, left, right]
    for peer in peers:
        pl.semaphore_signal(barrier, inc=1, device_id=peer, device_id_type=MESH)

    C[:, 0:2] = jnp.zeros((6, 2, CZ, LANES), BF)
    C[:, 18:20] = jnp.zeros((6, 2, CZ, LANES), BF)
    P3[:, 0:2] = jnp.zeros((6, 2, PITCH, LANES), BF)
    P3[:, 20:22] = jnp.zeros((6, 2, PITCH, LANES), BF)
    DF[SLAB * PLANE:, :] = jnp.zeros((SLAB * (PITCH - FZ), LANES), F32)

    loads[0].wait()
    line_row = lax.broadcasted_iota(jnp.int32, (PITCH, LANES), 0)

    def widen(i, _):
        rows = pl.ds(align(i * 4 * FZ * SLAB), 4 * FZ * SLAB)
        DF[rows, :] = raw[rows, :].astype(F32)
        return 0

    lax.fori_loop(0, FY // 4, widen, 0)

    def part(i, _):
        for x in range(SLAB):
            line = DF[pl.ds(i * FZ * SLAB + x, PITCH, stride=SLAB), :]
            D[x + 1, i] = jnp.where(line_row < FZ, line, 0.0).astype(BF)
        return 0

    lax.fori_loop(0, FY, part, 0)
    loads[1].wait()
    pl.semaphore_wait(barrier, len(peers))

    def halo(index, src, dst, peer):
        copy = pltpu.make_async_remote_copy(
            src_ref=src, dst_ref=dst, send_sem=halo_s.at[index], recv_sem=halo_r.at[index],
            device_id=peer, device_id_type=MESH,
        )
        copy.start()
        return copy

    halos = [
        halo(0, D.at[SLAB], D.at[0], right),
        halo(1, D.at[1], D.at[SLAB + 1], left),
        halo(2, C.at[SLAB, pl.ds(2, CY)], C.at[0, pl.ds(2, CY)], right),
        halo(3, C.at[1, pl.ds(2, CY)], C.at[SLAB + 1, pl.ds(2, CY)], left),
    ]

    zero_rows = jnp.zeros((LANES - 3 * MID, LANES), BF)
    for tap in range(TAPS):
        rows = pl.ds(tap * LANES, LANES)
        for src, straight, turned in ((win, W1, W1T), (wout, W2, W2T)):
            block = jnp.concatenate([src[tap], zero_rows], axis=0)
            straight[rows, :] = block
            turned[rows, :] = block.T
    AI[...] = jnp.zeros_like(AI)
    AO[...] = jnp.zeros_like(AO)
    WB[2 * GRAD:, :] = jnp.zeros((W_ROWS - 2 * GRAD, LANES), BF)
    FS[2 * PLANE:, :] = jnp.zeros((FIELD_PIECE - 2 * PLANE, LANES), F32)

    def lane_roll(values, count):
        count = count % LANES
        return pltpu.roll(values, count, 1) if count else values

    def row_roll(values, count):
        return pltpu.roll(values, count % values.shape[0], 0)

    def gather(values, direction):
        one = row_roll(lane_roll(values, -MID), -direction)
        two = row_roll(lane_roll(values, -2 * MID), -2 * direction)
        return values + one + two

    def spread(values, direction):
        one = row_roll(lane_roll(values, MID), -direction)
        two = row_roll(lane_roll(values, 2 * MID), -2 * direction)
        return values + one + two

    def first_mids(values):
        lane = lax.broadcasted_iota(jnp.int32, values.shape, 1)
        return jnp.where(lane < MID, values, 0.0)

    def stage_one(x):
        rows = HY * PITCH
        lhs = jnp.concatenate(
            [D[x + a, pl.ds(b, HY)].reshape(rows, LANES) for a in range(3) for b in range(3)], axis=1
        )
        pre = gather(jnp.dot(lhs, W1T[...], preferred_element_type=F32), 1)
        lhs = jnp.concatenate(
            [
                C[x + 2 - a, pl.ds(2 - b, HY)].reshape(HY * CZ, LANES)
                for a in range(3)
                for b in range(3)
            ],
            axis=1,
        )
        back = jnp.dot(lhs, W2T[...], preferred_element_type=F32).reshape(HY, CZ, LANES)
        back = jnp.concatenate([back, jnp.zeros((HY, PITCH - CZ, LANES), F32)], axis=1)
        grad = gather(back.reshape(rows, LANES), -1)
        square = pre * pre + 0.01
        inverse = lax.rsqrt(square)
        hidden = first_mids(0.505 * pre + 0.495 * (square * inverse))
        grad = first_mids(grad * (0.505 + 0.495 * (pre * inverse)))
        H3[x + 1] = spread(hidden, 1).reshape(HY, PITCH, LANES)[:, :CZ].astype(BF)
        P3[x + 1, pl.ds(2, HY)] = spread(grad, -1).reshape(HY, PITCH, LANES).astype(BF)
        return hidden, grad

    def inner_planes(i, _):
        stage_one(1 + i)
        return 0

    def outer_planes(i, _):
        hidden, grad = stage_one(3 * i)
        half = HALF * PITCH
        packed = hidden[:half] + lane_roll(hidden[half:], MID)
        packed = packed + lane_roll(grad[:half], 2 * MID) + lane_roll(grad[half:], 3 * MID)
        QS[i] = packed.astype(BF)
        return 0

    over_rows = (((0,), (0,)), ((), ()))

    def weight_terms(i):
        left_side = jnp.concatenate([H3[i + 1, pl.ds(b, CY)].reshape(CELLS, LANES) for b in range(3)], axis=1)
        right_side = jnp.concatenate(
            [C[i + 2 - a, pl.ds(2, CY)].reshape(CELLS, LANES) for a in range(3)], axis=1
        )
        AO[...] += lax.dot_general(left_side, right_side, over_rows, preferred_element_type=F32)
        left_side = jnp.concatenate(
            [P3[i + 1, pl.ds(2 - b, FY)].reshape(FY * PITCH, LANES) for b in range(3)], axis=1
        )
        right_side = jnp.concatenate([D[i + a].reshape(FY * PITCH, LANES) for a in range(3)], axis=1)
        AI[...] += lax.dot_general(left_side, right_side, over_rows, preferred_element_type=F32)

    def inner_weights(i, _):
        weight_terms(1 + i)
        return 0

    def outer_weights(i, _):
        weight_terms(3 * i)
        return 0

    lax.fori_loop(0, 2, inner_planes, 0)
    lax.fori_loop(0, 2, inner_weights, 0)
    for copy in halos[:4]:
        copy.wait_recv()
    lax.fori_loop(0, 2, outer_planes, 0)
    halos += [
        halo(4, QS.at[1], QR.at[0], right),
        halo(5, QS.at[0], QR.at[1], left),
    ]

    sends = []

    def send(src, dst, send_sem, recv_sem, peer):
        copy = pltpu.make_async_remote_copy(
            src_ref=src, dst_ref=dst, send_sem=send_sem, recv_sem=recv_sem, device_id=peer, device_id_type=MESH
        )
        copy.start()
        sends.append(copy)
        return copy

    def scatter(peers, piece, landing, size, sems):
        return [
            send(piece(align(place * size), size), landing(j), sems[0](j), sems[1](j), peer)
            for j, (peer, place) in enumerate(peers)
        ]

    def total(copies, piece, landing, me, size):
        for copy in copies:
            copy.wait_recv()
        value = piece(align(me * size), size)[...].astype(F32)
        for j in range(len(copies)):
            value = value + landing(j)[...].astype(F32)
        return value

    def spread_out(peers, whole, me, size, sems):
        rows = whole(align(me * size), size)
        return [send(rows, rows, sems[0](j), sems[1](j), peer) for j, (peer, _) in enumerate(peers)]

    class AfSum:
        def __init__(self, p):
            self.p, self.half, self.size = p, AF_ROWS[p] // 2, AF_ROWS[p] // 16
            self.base = AF_BASE[p] + core * self.half
            self.me = xl * 4 + y
            self.landing = (lambda j: land_out.at[p, j]) if p < 2 else (lambda j: land_field.at[p - 2, j])
            self.core_land = land_core.at[pl.ds(AF_BASE[p] // 2, self.half)]
            self.step = 0

        def piece(self, off, size):
            return B.at[pl.ds(align(self.base + off), size)]

        def whole(self, off, size):
            return R.at[pl.ds(align(self.base + off), size)]

        def advance(self):
            p, me, size = self.p, self.me, self.size
            if self.step == 0:
                give = B.at[pl.ds(align(AF_BASE[p] + (1 - core) * self.half), self.half)]
                self.copies = [send(give, self.core_land, core_s.at[p, 0], core_r.at[p, 0], other_core)]
            elif self.step == 1:
                self.copies[0].wait_recv()
                mine = self.piece(0, self.half)
                mine[...] = (mine[...].astype(F32) + self.core_land[...].astype(F32)).astype(BF)
                sems = (lambda j: rs_s.at[p, j], lambda j: rs_r.at[p, j])
                self.copies = scatter(af_peers, self.piece, self.landing, size, sems)
            elif self.step == 2:
                value = total(self.copies, self.piece, self.landing, me, size)
                value = value + EXTRA[pl.ds(align(self.base + me * size), size), :]
                self.whole(align(me * size), size)[...] = value.astype(BF)
                sems = (lambda j: ag_s.at[p, j], lambda j: ag_r.at[p, j])
                self.copies = spread_out(af_peers, self.whole, me, size, sems)
            elif self.step == 3:
                for copy in self.copies:
                    copy.wait_recv()
                rows = self.whole(0, self.half)
                self.copies = [send(rows, rows, core_s.at[p, 1], core_r.at[p, 1], other_core)]
            else:
                self.copies[0].wait_recv()
                rows = pl.ds(AF_BASE[p], AF_ROWS[p])
                store = pltpu.make_async_copy(R.at[rows], full_ref.at[rows], store_sem.at[p])
                store.start()
                stores.append(store)
            self.step += 1

    class GxSum:
        def __init__(self):
            self.me, self.size = xh * 4 + z, W_ROWS // 8
            self.step = 0

        def piece(self, off, size):
            return WB.at[pl.ds(off, size)]

        def whole(self, off, size):
            return WR.at[pl.ds(off, size)]

        def advance(self):
            me, size = self.me, self.size
            if self.step == 0:
                sems = (lambda j: ws_s.at[j], lambda j: ws_r.at[j])
                self.copies = scatter(gx_peers, self.piece, lambda j: land_w.at[j], size, sems)
            elif self.step == 1:
                value = total(self.copies, self.piece, lambda j: land_w.at[j], me, size)
                self.whole(align(me * size), size)[...] = value.astype(BF)
                sems = (lambda j: wg_s.at[j], lambda j: wg_r.at[j])
                self.copies = spread_out(gx_peers, self.whole, me, size, sems)
            else:
                for copy in self.copies:
                    copy.wait_recv()
                store = pltpu.make_async_copy(WR, grads_ref, store_sem.at[4])
                store.start()
                stores.append(store)
            self.step += 1

    stores = []
    out_a, out_b, field_a, field_b = [AfSum(p) for p in range(4)]
    grads = GxSum()

    lax.fori_loop(0, 2, outer_weights, 0)
    for acc, base in ((AI, 0), (AO, GRAD)):
        for a in range(3):
            for b in range(3):
                WB[pl.ds(base + (a * 3 + b) * 3 * MID, 3 * MID), :] = acc[
                    b * LANES : b * LANES + 3 * MID, a * LANES : (a + 1) * LANES
                ].astype(BF)
    grads.advance()

    def out_plane(slot):
        i = ORDER[slot]
        lhs = jnp.concatenate(
            [H3[i + a, pl.ds(b, CY)].reshape(CELLS, LANES) for a in range(3) for b in range(3)], axis=1
        )
        B[pl.ds(slot * CELLS, CELLS), :] = jnp.dot(lhs, W2[...], preferred_element_type=F32).astype(BF)

    def field_plane(slot):
        i = ORDER[slot]
        lhs = jnp.concatenate(
            [
                P3[i + 2 - a, pl.ds(2 - b, FY)].reshape(FY * PITCH, LANES)
                for a in range(3)
                for b in range(3)
            ],
            axis=1,
        )
        block = jnp.dot(lhs, W1[...], preferred_element_type=F32).reshape(FY, PITCH, LANES)
        for line in range(FY):
            FS[pl.ds((slot % 2) * PLANE + line * FZ, FZ), :] = block[line, :FZ]

    def field_rows(p):
        B[pl.ds(AF_BASE[p], FIELD_PIECE), :] = FS[...].astype(BF)

    def extra_out(i, _):
        for slot in range(SLAB):
            EXTRA[pl.ds(align(slot * CELLS + i * CZ), CZ), :] = DF[
                pl.ds((i + 2) * FZ * SLAB + 2 * SLAB + ORDER[slot], CZ, stride=SLAB), :
            ]
        return 0

    def extra_field():
        EXTRA[2 * OUT_PIECE:, :] = jnp.zeros((2 * FIELD_PIECE, LANES), F32)
        for slot in range(SLAB):
            base = 2 * OUT_PIECE + (slot // 2) * FIELD_PIECE + (slot % 2) * PLANE
            for line in range(CY):
                EXTRA[pl.ds(base + (line + 2) * FZ + 2, CZ), :] = C[ORDER[slot] + 1, line + 2].astype(F32)

    out_plane(0)
    out_plane(1)
    out_a.advance()
    field_plane(0)
    out_a.advance()
    field_plane(1)
    field_rows(2)
    field_a.advance()
    lax.fori_loop(0, CY, extra_out, 0)
    extra_field()
    field_a.advance()

    for copy in halos[4:6]:
        copy.wait_recv()

    def unpack(i, _):
        packed = QR[i].astype(F32)
        for r in range(2):
            hidden = first_mids(lane_roll(packed, -r * MID))
            grad = first_mids(lane_roll(packed, -(2 + r) * MID))
            hidden = spread(hidden, 1).reshape(HALF, PITCH, LANES)[:, :CZ]
            H3[5 * i, pl.ds(r * HALF, HALF)] = hidden.astype(BF)
            grad = spread(grad, -1).reshape(HALF, PITCH, LANES)
            P3[5 * i, pl.ds(2 + r * HALF, HALF)] = grad.astype(BF)
        return 0

    lax.fori_loop(0, 2, unpack, 0)
    out_plane(2)
    out_plane(3)
    out_b.advance()
    out_a.advance()
    field_plane(2)
    out_b.advance()
    field_a.advance()
    field_plane(3)
    field_rows(3)
    field_b.advance()
    grads.advance()
    field_b.advance()
    out_b.advance()
    out_a.advance()
    field_a.advance()
    field_b.advance()
    out_b.advance()
    grads.advance()
    out_a.advance()
    field_a.advance()
    out_b.advance()
    field_b.advance()
    field_b.advance()
    for store in stores:
        store.wait()
    for copy in halos + sends:
        copy.wait_send()


def finish(full, grads, out_ref, field_ref, inner_ref, outer_ref, f_in, g_in, f_out, w_out, in_sem, out_sem):
    lines = 4
    steps = FY // lines
    rows = lines * FZ

    def source(step, slot):
        base = 2 * OUT_PIECE + (slot // 2) * FIELD_PIECE + (slot % 2) * PLANE
        return pltpu.make_async_copy(
            full.at[pl.ds(base + step * rows, rows)], f_in.at[step, slot], in_sem.at[step, slot]
        )

    inputs = [[source(step, slot) for slot in range(SLAB)] for step in range(steps)]
    whole = pltpu.make_async_copy(grads, g_in, in_sem.at[steps, 0])
    for copies in inputs:
        for copy in copies:
            copy.start()
    whole.start()
    stores = []

    def store(src, dst):
        copy = pltpu.make_async_copy(src, dst, out_sem.at[len(stores)])
        copy.start()
        stores.append(copy)

    for slot in range(SLAB):
        store(full.at[pl.ds(slot * CELLS, CELLS)], out_ref.at[pl.ds(ORDER[slot] * CELLS, CELLS)])
    for step in range(steps):
        for slot in range(SLAB):
            inputs[step][slot].wait()
            f_out[pl.ds(step * rows * SLAB + ORDER[slot], rows, stride=SLAB), :] = f_in[step, slot].astype(F32)
        part = pl.ds(step * rows * SLAB, rows * SLAB)
        store(f_out.at[part], field_ref.at[part])
    whole.wait()
    for p, ref in enumerate((inner_ref, outer_ref)):
        part = pl.ds(p * GRAD, GRAD)
        w_out[part, :] = g_in[part, :].astype(F32)
        store(w_out.at[part], ref)
    for copy in stores:
        copy.wait()


def shards(displace, weight_in, weight_out, cotangent):
    vmem = pl.BlockSpec(memory_space=pltpu.VMEM)
    hbm = pl.BlockSpec(memory_space=pl.ANY)
    rows = jnp.transpose(displace, (1, 2, 0, 3)).reshape(SLAB * PLANE, LANES)
    win = jnp.transpose(weight_in, (0, 1, 2, 4, 3)).reshape(TAPS, 3 * MID, LANES)
    wout = weight_out.reshape(TAPS, 3 * MID, LANES)
    dma = pltpu.SemaphoreType.DMA
    full, grads = pl.pallas_call(
        kernel,
        out_shape=(
            jax.ShapeDtypeStruct((AF_TOTAL, LANES), BF),
            jax.ShapeDtypeStruct((W_ROWS, LANES), BF),
        ),
        in_specs=[hbm, hbm, vmem, vmem],
        out_specs=[hbm] * 2,
        scratch_shapes=[
            pltpu.VMEM((SLAB * PLANE, LANES), BF),
            pltpu.VMEM((SLAB + 2, FY, PITCH, LANES), BF),
            pltpu.VMEM((SLAB + 2, FY, CZ, LANES), BF),
            pltpu.VMEM((SLAB + 2, HY, CZ, LANES), BF),
            pltpu.VMEM((SLAB + 2, HY + 4, PITCH, LANES), BF),
            pltpu.VMEM((TAPS * LANES, LANES), BF),
            pltpu.VMEM((TAPS * LANES, LANES), BF),
            pltpu.VMEM((TAPS * LANES, LANES), BF),
            pltpu.VMEM((TAPS * LANES, LANES), BF),
            pltpu.VMEM((3 * LANES, 3 * LANES), F32),
            pltpu.VMEM((3 * LANES, 3 * LANES), F32),
            pltpu.VMEM((SLAB * (PLANE + PITCH - FZ), LANES), F32),
            pltpu.VMEM((FIELD_PIECE, LANES), F32),
            pltpu.VMEM((AF_TOTAL, LANES), F32),
            pltpu.VMEM((AF_TOTAL, LANES), BF),
            pltpu.VMEM((AF_TOTAL, LANES), BF),
            pltpu.VMEM((W_ROWS, LANES), BF),
            pltpu.VMEM((W_ROWS, LANES), BF),
            pltpu.VMEM((2, HALF * PITCH, LANES), BF),
            pltpu.VMEM((2, HALF * PITCH, LANES), BF),
            pltpu.VMEM((AF_TOTAL // 2, LANES), BF),
            pltpu.VMEM((2, 7, OUT_PIECE // 16, LANES), BF),
            pltpu.VMEM((2, 7, FIELD_PIECE // 16, LANES), BF),
            pltpu.VMEM((7, W_ROWS // 8, LANES), BF),
            dma((2,)), dma((6,)), dma((6,)),
            dma((4, 2)), dma((4, 2)), dma((4, 7)), dma((4, 7)), dma((4, 7)), dma((4, 7)),
            dma((7,)), dma((7,)), dma((7,)), dma((7,)), dma((5,)),
        ],
        compiler_params=pltpu.CompilerParams(
            collective_id=0, has_side_effects=True, vmem_limit_bytes=48 * 1024 * 1024
        ),
        cost_estimate=pl.CostEstimate(flops=4_000_000_000, bytes_accessed=8_000_000, transcendentals=400_000),
    )(rows, cotangent, win, wout)
    out, field, inner, outer = pl.pallas_call(
        finish,
        out_shape=(
            jax.ShapeDtypeStruct((SLAB * CELLS, LANES), BF),
            jax.ShapeDtypeStruct((SLAB * PLANE, LANES), F32),
            jax.ShapeDtypeStruct((GRAD, LANES), F32),
            jax.ShapeDtypeStruct((GRAD, LANES), F32),
        ),
        in_specs=[hbm] * 2,
        out_specs=[hbm] * 4,
        scratch_shapes=[
            pltpu.VMEM((5, SLAB, 4 * FZ, LANES), BF),
            pltpu.VMEM((W_ROWS, LANES), BF),
            pltpu.VMEM((SLAB * PLANE, LANES), F32),
            pltpu.VMEM((2 * GRAD, LANES), F32),
            dma((6, SLAB)), dma((11,)),
        ],
        compiler_params=pltpu.CompilerParams(vmem_limit_bytes=16 * 1024 * 1024),
        cost_estimate=pl.CostEstimate(flops=0, bytes_accessed=5_000_000, transcendentals=0),
    )(full, grads)
    out_field = out.reshape(SLAB, CY, CZ, LANES)
    field_grad = jnp.transpose(field.reshape(FY, FZ, SLAB, LANES), (2, 0, 1, 3))
    inner_grad = jnp.transpose(inner.reshape(3, 3, 3, MID, LANES), (0, 1, 2, 4, 3))
    outer_grad = outer.reshape(3, 3, 3, MID, LANES)
    return (out_field, field_grad, inner_grad, outer_grad)


def solution(mesh):
    return jax.shard_map(
        shards,
        mesh=mesh,
        in_specs=(
            P("gx", None, None, None),
            P(None, None, None, None, "af"),
            P(None, None, None, "af", None),
            P("gx", None, None, None),
        ),
        out_specs=(
            P("gx", None, None, None),
            P("gx", None, None, None),
            P(None, None, None, None, "af"),
            P(None, None, None, "af", None),
        ),
        check_vma=False,
    )
```

profile of v0, /device:TPU:1, one launch (start us, length us, event | category | flops | bytes accessed | tf_op | source)
XLA Modules:
  0.0 64.9 jit_solution(15947450692837868572)
XLA Ops:
  0.6 0.0 copy-start
  0.6 1.1 %copy-done = bf16[4,20,36,128]{3,0,2,1:T(4,128)(2,1)S(1)} copy-done((bf16[4,20,36,128]{3,0,2,1:T(4,128)(2,1)S(1)}, bf16[4,20,36,128]{3,0,2,1:T(4,128)(2,1)}, u32[]{:S(2)}) %copy-start) | copy-done | bytes 737304
  1.7 0.0 copy-start.1
  1.8 1.0 %copy-done.1 = bf16[4,16,32,128]{3,2,1,0:T(8,128)(2,1)S(1)} copy-done((bf16[4,16,32,128]{3,2,1,0:T(8,128)(2,1)S(1)}, bf16[4,16,32,128]{3,2,1,0:T(8,128)(2,1)}, u32[]{:S(2)}) %copy-start.1) | copy-done | bytes 524312
  2.8 0.0 copy-start.2
  2.8 0.9 %copy-done.2 = bf16[3,3,3,128,32]{3,4,2,1,0:T(8,128)(2,1)S(1)} copy-done((bf16[3,3,3,128,32]{3,4,2,1,0:T(8,128)(2,1)S(1)}, bf16[3,3,3,128,32]{3,4,2,1,0:T(8,128)(2,1)}, u32[]{:S(2)}) %copy-start.2) | copy-done | bytes 221208
  3.7 0.0 copy-start.3
  3.7 0.9 %copy-done.3 = bf16[3,3,3,32,128]{4,3,2,1,0:T(8,128)(2,1)S(1)} copy-done((bf16[3,3,3,32,128]{4,3,2,1,0:T(8,128)(2,1)S(1)}, bf16[3,3,3,32,128]{4,3,2,1,0:T(8,128)(2,1)}, u32[]{:S(2)}) %copy-start.3) | copy-done | bytes 221208
  4.7 57.1 %shard_map.75 = (bf16[5120,128]{1,0:T(8,128)(2,1)S(1)}, bf16[1792,128]{1,0:T(8,128)(2,1)S(1)}) custom-call(bf16[2880,128]{1,0:T(8,128)(2,1)S(1)} %bitcast.15, bf16[4,16,32,128]{3,2,1,0:T(8,128)(2,1)S(1)} %copy-done.1, bf16[9,96,128]{2,1,0:T(8,128)(2,1)S(1)} %bitcast.16, bf16[9,96,128]{2,1,0:T(8,128)(2,1)S(1)} %bitcast.17), custom_call_target="tpu_custom_call" | custom-call | flops 4000000000 | bytes 8000000 | tf_op jit(solution)/shard_map/pallas_call | solution.py:474
  61.8 3.1 %shard_map.76 = (bf16[2048,128]{1,0:T(8,128)(2,1)}, f32[2880,128]{1,0:T(8,128)}, f32[864,128]{1,0:T(8,128)}, f32[864,128]{1,0:T(8,128)}) custom-call(bf16[5120,128]{1,0:T(8,128)(2,1)S(1)} %get-tuple-element.10.full, bf16[1792,128]{1,0:T(8,128)(2,1)S(1)} %get-tuple-element.11.grads), custom_call_target="tpu_custom_call" | custom-call | bytes 5000000 | tf_op jit(solution)/shard_map/pallas_call | solution.py:516
Async XLA Ops:
  0.6 1.1 %copy-start = (bf16[4,20,36,128]{3,0,2,1:T(4,128)(2,1)S(1)}, bf16[4,20,36,128]{3,0,2,1:T(4,128)(2,1)}, u32[]{:S(2)}) copy-start(bf16[4,20,36,128]{3,0,2,1:T(4,128)(2,1)} %param.4) | copy-start | bytes 2211844
  1.7 1.0 %copy-start.1 = (bf16[4,16,32,128]{3,2,1,0:T(8,128)(2,1)S(1)}, bf16[4,16,32,128]{3,2,1,0:T(8,128)(2,1)}, u32[]{:S(2)}) copy-start(bf16[4,16,32,128]{3,2,1,0:T(8,128)(2,1)} %cot.1) | copy-start | bytes 1572868
  2.8 0.9 %copy-start.2 = (bf16[3,3,3,128,32]{3,4,2,1,0:T(8,128)(2,1)S(1)}, bf16[3,3,3,128,32]{3,4,2,1,0:T(8,128)(2,1)}, u32[]{:S(2)}) copy-start(bf16[3,3,3,128,32]{3,4,2,1,0:T(8,128)(2,1)} %param.5) | copy-start | bytes 663556
  3.7 0.9 %copy-start.3 = (bf16[3,3,3,32,128]{4,3,2,1,0:T(8,128)(2,1)S(1)}, bf16[3,3,3,32,128]{4,3,2,1,0:T(8,128)(2,1)}, u32[]{:S(2)}) copy-start(bf16[3,3,3,32,128]{4,3,2,1,0:T(8,128)(2,1)} %param.6) | copy-start | bytes 663556
where the time goes:
time: 65.1 us; the launch traced here: 64.9 us
  Pallas kernels  60.2 us (92%)
  local copies, waits for them, and re-layouts  4.02 us (6%)
    pallas_call x1, Pallas kernels, shards(): pl.pallas_call(kernel, out_shape=(jax.ShapeDtypeStruct((AF_TOTAL, LANES),...  57.1 us
    unnamed x8, local copies, waits for them, and re-layouts  4.02 us
    pallas_call x1, Pallas kernels, shards(): pl.pallas_call(finish, out_shape=(jax.ShapeDtypeStruct((SLAB * CELLS, LAN...  3.1 us

commit v1 on v0

--- a/solution.py
+++ b/solution.py
@@ -22,12 +22,16 @@
 ORDER = (1, 2, 0, 3)
 
 OUT_PIECE = 2 * CELLS
-FIELD_PIECE = 1536
-AF_ROWS = (OUT_PIECE, OUT_PIECE, FIELD_PIECE, FIELD_PIECE)
-AF_BASE = (0, OUT_PIECE, 2 * OUT_PIECE, 2 * OUT_PIECE + FIELD_PIECE)
+FIELD_SLOT = 768
+FIELD_BASE = 2 * OUT_PIECE
+AF_ROWS = (OUT_PIECE, OUT_PIECE, 2 * FIELD_SLOT, FIELD_SLOT, FIELD_SLOT)
+AF_BASE = tuple(sum(AF_ROWS[:p]) for p in range(5))
 AF_TOTAL = sum(AF_ROWS)
+AF_LAND = tuple(7 * base // 16 for base in AF_BASE)
+HALO = 368
 GRAD = 3 * TAPS * MID
 W_ROWS = 1792
+W_PART = W_ROWS // 4
 
 
 def align(value, by=16):
@@ -37,9 +41,9 @@
 def kernel(
     disp, cot, win, wout,
     full_ref, grads_ref,
-    raw, D, C, H3, P3, W1T, W1, W2T, W2, AI, AO, DF, FS, EXTRA, B, R, WB, WR, QS, QR,
-    land_core, land_out, land_field, land_w,
-    load_sem, halo_s, halo_r, core_s, core_r, rs_s, rs_r, ag_s, ag_r, ws_s, ws_r, wg_s, wg_r, store_sem,
+    raw, D, C, H3, P3, W1T, W1, W2T, W2, AI, AO, DF, FS, EXTRA, B, R, WB, WZ, WR, QS, QR, HS, HL, HF,
+    land_core, land_af, land_z, land_x,
+    load_sem, halo_s, halo_r, core_s, core_r, rs_s, rs_r, ag_s, ag_r, ws_s, ws_r, wx_s, wx_r, wg_s, wg_r, store_sem,
 ):
     gx = lax.axis_index("gx")
     af = lax.axis_index("af")
@@ -49,13 +53,14 @@
     z = lax.rem(gx, 4)
     xh = lax.div(gx, 4)
 
-    order = ((1, 2), (0, 2), (1, 1), (1, 3), (0, 1), (0, 3), (1, 0))
-    af_peers, gx_peers = [], []
-    for dx, dy in order:
+    af_peers, z_peers = [], []
+    for dx, dy in ((1, 2), (0, 2), (1, 1), (1, 3), (0, 1), (0, 3), (1, 0)):
         x2, y2 = lax.rem(xl + dx, 2), lax.rem(y + dy, 4)
         af_peers.append(((gx, (x2 * 4 + y2) * 2 + core), x2 * 4 + y2))
-        x2, z2 = lax.rem(xh + dx, 2), lax.rem(z + dy, 4)
-        gx_peers.append(((x2 * 4 + z2, af), x2 * 4 + z2))
+    for dz in (2, 1, 3):
+        z2 = lax.rem(z + dz, 4)
+        z_peers.append(((xh * 4 + z2, af), z2))
+    x_peer = ((1 - xh) * 4 + z, af)
     other_core = (gx, af + 1 - 2 * core)
     right = (lax.rem(gx + 1, 8), af)
     left = (lax.rem(gx + 7, 8), af)
@@ -63,11 +68,13 @@
     loads = [
         pltpu.make_async_copy(disp, raw, load_sem.at[0]),
         pltpu.make_async_copy(cot, C.at[pl.ds(1, SLAB), pl.ds(2, CY)], load_sem.at[1]),
+        pltpu.make_async_copy(win, W1.at[:, pl.ds(0, 3 * MID)], load_sem.at[2]),
+        pltpu.make_async_copy(wout, W2.at[:, pl.ds(0, 3 * MID)], load_sem.at[3]),
     ]
     for load in loads:
         load.start()
     barrier = pltpu.get_barrier_semaphore()
-    peers = [peer for peer, _ in af_peers + gx_peers] + [other_core, left, right]
+    peers = [peer for peer, _ in af_peers + z_peers] + [x_peer, other_core, left, right]
     for peer in peers:
         pl.semaphore_signal(barrier, inc=1, device_id=peer, device_id_type=MESH)
 
@@ -76,6 +83,14 @@
     P3[:, 0:2] = jnp.zeros((6, 2, PITCH, LANES), BF)
     P3[:, 20:22] = jnp.zeros((6, 2, PITCH, LANES), BF)
     DF[SLAB * PLANE:, :] = jnp.zeros((SLAB * (PITCH - FZ), LANES), F32)
+    HF[PLANE:, :] = jnp.zeros((16, LANES), F32)
+    zero_rows = jnp.zeros((TAPS, LANES - 3 * MID, LANES), BF)
+    W1[:, 3 * MID:] = zero_rows
+    W2[:, 3 * MID:] = zero_rows
+    AI[...] = jnp.zeros_like(AI)
+    AO[...] = jnp.zeros_like(AO)
+    WB[2 * GRAD:, :] = jnp.zeros((W_ROWS - 2 * GRAD, LANES), BF)
+    FS[2 * PLANE:, :] = jnp.zeros((2 * FIELD_SLOT - 2 * PLANE, LANES), F32)
 
     loads[0].wait()
     line_row = lax.broadcasted_iota(jnp.int32, (PITCH, LANES), 0)
@@ -86,6 +101,8 @@
         return 0
 
     lax.fori_loop(0, FY // 4, widen, 0)
+    for side, x in enumerate((0, SLAB - 1)):
+        HS[side] = DF[pl.ds(x, PLANE, stride=SLAB), :].astype(BF)
 
     def part(i, _):
         for x in range(SLAB):
@@ -94,35 +111,11 @@
         return 0
 
     lax.fori_loop(0, FY, part, 0)
-    loads[1].wait()
-    pl.semaphore_wait(barrier, len(peers))
-
-    def halo(index, src, dst, peer):
-        copy = pltpu.make_async_remote_copy(
-            src_ref=src, dst_ref=dst, send_sem=halo_s.at[index], recv_sem=halo_r.at[index],
-            device_id=peer, device_id_type=MESH,
-        )
-        copy.start()
-        return copy
-
-    halos = [
-        halo(0, D.at[SLAB], D.at[0], right),
-        halo(1, D.at[1], D.at[SLAB + 1], left),
-        halo(2, C.at[SLAB, pl.ds(2, CY)], C.at[0, pl.ds(2, CY)], right),
-        halo(3, C.at[1, pl.ds(2, CY)], C.at[SLAB + 1, pl.ds(2, CY)], left),
-    ]
-
-    zero_rows = jnp.zeros((LANES - 3 * MID, LANES), BF)
-    for tap in range(TAPS):
-        rows = pl.ds(tap * LANES, LANES)
-        for src, straight, turned in ((win, W1, W1T), (wout, W2, W2T)):
-            block = jnp.concatenate([src[tap], zero_rows], axis=0)
-            straight[rows, :] = block
-            turned[rows, :] = block.T
-    AI[...] = jnp.zeros_like(AI)
-    AO[...] = jnp.zeros_like(AO)
-    WB[2 * GRAD:, :] = jnp.zeros((W_ROWS - 2 * GRAD, LANES), BF)
-    FS[2 * PLANE:, :] = jnp.zeros((FIELD_PIECE - 2 * PLANE, LANES), F32)
+    for load in loads[1:]:
+        load.wait()
+    for straight, turned in ((W1, W1T), (W2, W2T)):
+        for tap in range(TAPS):
+            turned[pl.ds(tap * LANES, LANES), :] = straight[tap].T
 
     def lane_roll(values, count):
         count = count % LANES
@@ -170,17 +163,12 @@
         P3[x + 1, pl.ds(2, HY)] = spread(grad, -1).reshape(HY, PITCH, LANES).astype(BF)
         return hidden, grad
 
-    def inner_planes(i, _):
-        stage_one(1 + i)
-        return 0
-
-    def outer_planes(i, _):
+    def outer_plane(i):
         hidden, grad = stage_one(3 * i)
         half = HALF * PITCH
         packed = hidden[:half] + lane_roll(hidden[half:], MID)
         packed = packed + lane_roll(grad[:half], 2 * MID) + lane_roll(grad[half:], 3 * MID)
         QS[i] = packed.astype(BF)
-        return 0
 
     over_rows = (((0,), (0,)), ((), ()))
 
@@ -204,15 +192,49 @@
         weight_terms(3 * i)
         return 0
 
-    lax.fori_loop(0, 2, inner_planes, 0)
+    def halo(index, src, dst, peer):
+        copy = pltpu.make_async_remote_copy(
+            src_ref=src, dst_ref=dst, send_sem=halo_s.at[index], recv_sem=halo_r.at[index],
+            device_id=peer, device_id_type=MESH,
+        )
+        copy.start()
+        halos.append(copy)
+        return copy
+
+    halos = []
+    mine = pl.ds(align(core * 352), HALO)
+    my_lines = pl.ds(2 + core * (CY // 2), CY // 2)
+    stage_one(1)
+    pl.semaphore_wait(barrier, len(peers))
+    first_halos = [
+        halo(0, HS.at[1, mine], HL.at[0, core], right),
+        halo(1, HS.at[0, mine], HL.at[1, core], left),
+        halo(2, C.at[SLAB, my_lines], C.at[0, my_lines], right),
+        halo(3, C.at[1, my_lines], C.at[SLAB + 1, my_lines], left),
+    ]
+    stage_one(2)
     lax.fori_loop(0, 2, inner_weights, 0)
-    for copy in halos[:4]:
-        copy.wait_recv()
-    lax.fori_loop(0, 2, outer_planes, 0)
-    halos += [
-        halo(4, QS.at[1], QR.at[0], right),
-        halo(5, QS.at[0], QR.at[1], left),
-    ]
+    shares = []
+    for side in range(2):
+        first_halos[side].wait_recv()
+        shares.append(halo(4 + side, HL.at[side, core], HL.at[side, core], other_core))
+    for side in range(2):
+        first_halos[2 + side].wait_recv()
+        rows = C.at[side * (SLAB + 1), my_lines]
+        shares.append(halo(6 + side, rows, rows, other_core))
+    for side in range(2):
+        shares[side].wait_recv()
+        HF[0:HALO, :] = HL[side, 0].astype(F32)
+        HF[PLANE - HALO : PLANE, :] = HL[side, 1].astype(F32)
+        for line in range(FY):
+            value = HF[pl.ds(line * FZ, PITCH), :]
+            D[side * (SLAB + 1), line] = jnp.where(line_row < FZ, value, 0.0).astype(BF)
+    for side in range(2):
+        shares[2 + side].wait_recv()
+    outer_plane(0)
+    second_halos = [halo(8, QS.at[0], QR.at[1], left)]
+    outer_plane(1)
+    second_halos.append(halo(9, QS.at[1], QR.at[0], right))
 
     sends = []
 
@@ -247,7 +269,7 @@
             self.p, self.half, self.size = p, AF_ROWS[p] // 2, AF_ROWS[p] // 16
             self.base = AF_BASE[p] + core * self.half
             self.me = xl * 4 + y
-            self.landing = (lambda j: land_out.at[p, j]) if p < 2 else (lambda j: land_field.at[p - 2, j])
+            self.landing = lambda j: land_af.at[pl.ds(AF_LAND[p] + j * self.size, self.size)]
             self.core_land = land_core.at[pl.ds(AF_BASE[p] // 2, self.half)]
             self.step = 0
 
@@ -289,7 +311,6 @@
 
     class GxSum:
         def __init__(self):
-            self.me, self.size = xh * 4 + z, W_ROWS // 8
             self.step = 0
 
         def piece(self, off, size):
@@ -299,25 +320,28 @@
             return WR.at[pl.ds(off, size)]
 
         def advance(self):
-            me, size = self.me, self.size
             if self.step == 0:
                 sems = (lambda j: ws_s.at[j], lambda j: ws_r.at[j])
-                self.copies = scatter(gx_peers, self.piece, lambda j: land_w.at[j], size, sems)
+                self.copies = scatter(z_peers, self.piece, lambda j: land_z.at[j], W_PART, sems)
             elif self.step == 1:
-                value = total(self.copies, self.piece, lambda j: land_w.at[j], me, size)
-                self.whole(align(me * size), size)[...] = value.astype(BF)
+                WZ[...] = total(self.copies, self.piece, lambda j: land_z.at[j], z, W_PART).astype(BF)
+                self.copies = [send(WZ, land_x, wx_s.at[0], wx_r.at[0], x_peer)]
+            elif self.step == 2:
+                self.copies[0].wait_recv()
+                value = WZ[...].astype(F32) + land_x[...].astype(F32)
+                self.whole(align(z * W_PART), W_PART)[...] = value.astype(BF)
                 sems = (lambda j: wg_s.at[j], lambda j: wg_r.at[j])
-                self.copies = spread_out(gx_peers, self.whole, me, size, sems)
+                self.copies = spread_out(z_peers, self.whole, z, W_PART, sems)
             else:
                 for copy in self.copies:
                     copy.wait_recv()
-                store = pltpu.make_async_copy(WR, grads_ref, store_sem.at[4])
+                store = pltpu.make_async_copy(WR, grads_ref, store_sem.at[5])
                 store.start()
                 stores.append(store)
             self.step += 1
 
     stores = []
-    out_a, out_b, field_a, field_b = [AfSum(p) for p in range(4)]
+    out_a, out_b, field_a, field_b, field_c = [AfSum(p) for p in range(5)]
     grads = GxSum()
 
     lax.fori_loop(0, 2, outer_weights, 0)
@@ -334,7 +358,8 @@
         lhs = jnp.concatenate(
             [H3[i + a, pl.ds(b, CY)].reshape(CELLS, LANES) for a in range(3) for b in range(3)], axis=1
         )
-        B[pl.ds(slot * CELLS, CELLS), :] = jnp.dot(lhs, W2[...], preferred_element_type=F32).astype(BF)
+        weights = W2[...].reshape(TAPS * LANES, LANES)
+        B[pl.ds(slot * CELLS, CELLS), :] = jnp.dot(lhs, weights, preferred_element_type=F32).astype(BF)
 
     def field_plane(slot):
         i = ORDER[slot]
@@ -346,12 +371,12 @@
             ],
             axis=1,
         )
-        block = jnp.dot(lhs, W1[...], preferred_element_type=F32).reshape(FY, PITCH, LANES)
+        weights = W1[...].reshape(TAPS * LANES, LANES)
+        block = jnp.dot(lhs, weights, preferred_element_type=F32).reshape(FY, PITCH, LANES)
+        base = (slot % 2) * FIELD_SLOT
         for line in range(FY):
-            FS[pl.ds((slot % 2) * PLANE + line * FZ, FZ), :] = block[line, :FZ]
-
-    def field_rows(p):
-        B[pl.ds(AF_BASE[p], FIELD_PIECE), :] = FS[...].astype(BF)
+            FS[pl.ds(base + line * FZ, FZ), :] = block[line, :FZ]
+        B[pl.ds(FIELD_BASE + slot * FIELD_SLOT, FIELD_SLOT), :] = FS[pl.ds(base, FIELD_SLOT), :].astype(BF)
 
     def extra_out(i, _):
         for slot in range(SLAB):
@@ -361,9 +386,9 @@
         return 0
 
     def extra_field():
-        EXTRA[2 * OUT_PIECE:, :] = jnp.zeros((2 * FIELD_PIECE, LANES), F32)
+        EXTRA[FIELD_BASE:, :] = jnp.zeros((SLAB * FIELD_SLOT, LANES), F32)
         for slot in range(SLAB):
-            base = 2 * OUT_PIECE + (slot // 2) * FIELD_PIECE + (slot % 2) * PLANE
+            base = FIELD_BASE + slot * FIELD_SLOT
             for line in range(CY):
                 EXTRA[pl.ds(base + (line + 2) * FZ + 2, CZ), :] = C[ORDER[slot] + 1, line + 2].astype(F32)
 
@@ -373,13 +398,12 @@
     field_plane(0)
     out_a.advance()
     field_plane(1)
-    field_rows(2)
     field_a.advance()
     lax.fori_loop(0, CY, extra_out, 0)
     extra_field()
     field_a.advance()
 
-    for copy in halos[4:6]:
+    for copy in second_halos:
         copy.wait_recv()
 
     def unpack(i, _):
@@ -397,26 +421,31 @@
     out_plane(2)
     out_plane(3)
     out_b.advance()
+    field_plane(2)
+    field_b.advance()
+    out_b.advance()
+    field_plane(3)
+    field_c.advance()
+    field_b.advance()
+    field_c.advance()
     out_a.advance()
-    field_plane(2)
+    grads.advance()
+    field_a.advance()
     out_b.advance()
+    field_b.advance()
+    field_c.advance()
+    grads.advance()
+    out_a.advance()
     field_a.advance()
-    field_plane(3)
-    field_rows(3)
-    field_b.advance()
-    grads.advance()
-    field_b.advance()
     out_b.advance()
     out_a.advance()
     field_a.advance()
     field_b.advance()
     out_b.advance()
+    field_c.advance()
     grads.advance()
-    out_a.advance()
-    field_a.advance()
-    out_b.advance()
     field_b.advance()
-    field_b.advance()
+    field_c.advance()
     for store in stores:
         store.wait()
     for copy in halos + sends:
@@ -429,7 +458,7 @@
     rows = lines * FZ
 
     def source(step, slot):
-        base = 2 * OUT_PIECE + (slot // 2) * FIELD_PIECE + (slot % 2) * PLANE
+        base = FIELD_BASE + slot * FIELD_SLOT
         return pltpu.make_async_copy(
             full.at[pl.ds(base + step * rows, rows)], f_in.at[step, slot], in_sem.at[step, slot]
         )
@@ -465,7 +494,6 @@
 
 
 def shards(displace, weight_in, weight_out, cotangent):
-    vmem = pl.BlockSpec(memory_space=pltpu.VMEM)
     hbm = pl.BlockSpec(memory_space=pl.ANY)
     rows = jnp.transpose(displace, (1, 2, 0, 3)).reshape(SLAB * PLANE, LANES)
     win = jnp.transpose(weight_in, (0, 1, 2, 4, 3)).reshape(TAPS, 3 * MID, LANES)
@@ -477,7 +505,7 @@
             jax.ShapeDtypeStruct((AF_TOTAL, LANES), BF),
             jax.ShapeDtypeStruct((W_ROWS, LANES), BF),
         ),
-        in_specs=[hbm, hbm, vmem, vmem],
+        in_specs=[pl.BlockSpec(memory_space=pltpu.HBM)] * 4,
         out_specs=[hbm] * 2,
         scratch_shapes=[
             pltpu.VMEM((SLAB * PLANE, LANES), BF),
@@ -486,30 +514,34 @@
             pltpu.VMEM((SLAB + 2, HY, CZ, LANES), BF),
             pltpu.VMEM((SLAB + 2, HY + 4, PITCH, LANES), BF),
             pltpu.VMEM((TAPS * LANES, LANES), BF),
+            pltpu.VMEM((TAPS, LANES, LANES), BF),
             pltpu.VMEM((TAPS * LANES, LANES), BF),
-            pltpu.VMEM((TAPS * LANES, LANES), BF),
-            pltpu.VMEM((TAPS * LANES, LANES), BF),
+            pltpu.VMEM((TAPS, LANES, LANES), BF),
             pltpu.VMEM((3 * LANES, 3 * LANES), F32),
             pltpu.VMEM((3 * LANES, 3 * LANES), F32),
             pltpu.VMEM((SLAB * (PLANE + PITCH - FZ), LANES), F32),
-            pltpu.VMEM((FIELD_PIECE, LANES), F32),
+            pltpu.VMEM((2 * FIELD_SLOT, LANES), F32),
             pltpu.VMEM((AF_TOTAL, LANES), F32),
             pltpu.VMEM((AF_TOTAL, LANES), BF),
             pltpu.VMEM((AF_TOTAL, LANES), BF),
             pltpu.VMEM((W_ROWS, LANES), BF),
+            pltpu.VMEM((W_PART, LANES), BF),
             pltpu.VMEM((W_ROWS, LANES), BF),
             pltpu.VMEM((2, HALF * PITCH, LANES), BF),
             pltpu.VMEM((2, HALF * PITCH, LANES), BF),
+            pltpu.VMEM((2, PLANE, LANES), BF),
+            pltpu.VMEM((2, 2, HALO, LANES), BF),
+            pltpu.VMEM((PLANE + 16, LANES), F32),
             pltpu.VMEM((AF_TOTAL // 2, LANES), BF),
-            pltpu.VMEM((2, 7, OUT_PIECE // 16, LANES), BF),
-            pltpu.VMEM((2, 7, FIELD_PIECE // 16, LANES), BF),
-            pltpu.VMEM((7, W_ROWS // 8, LANES), BF),
-            dma((2,)), dma((6,)), dma((6,)),
-            dma((4, 2)), dma((4, 2)), dma((4, 7)), dma((4, 7)), dma((4, 7)), dma((4, 7)),
-            dma((7,)), dma((7,)), dma((7,)), dma((7,)), dma((5,)),
+            pltpu.VMEM((7 * AF_TOTAL // 16, LANES), BF),
+            pltpu.VMEM((3, W_PART, LANES), BF),
+            pltpu.VMEM((W_PART, LANES), BF),
+            dma((4,)), dma((10,)), dma((10,)),
+            dma((5, 2)), dma((5, 2)), dma((5, 7)), dma((5, 7)), dma((5, 7)), dma((5, 7)),
+            dma((3,)), dma((3,)), dma((1,)), dma((1,)), dma((3,)), dma((3,)), dma((6,)),
         ],
         compiler_params=pltpu.CompilerParams(
-            collective_id=0, has_side_effects=True, vmem_limit_bytes=48 * 1024 * 1024
+            collective_id=0, has_side_effects=True, vmem_limit_bytes=56 * 1024 * 1024
         ),
         cost_estimate=pl.CostEstimate(flops=4_000_000_000, bytes_accessed=8_000_000, transcendentals=400_000),
     )(rows, cotangent, win, wout)
@@ -530,7 +562,7 @@
             pltpu.VMEM((2 * GRAD, LANES), F32),
             dma((6, SLAB)), dma((11,)),
         ],
-        compiler_params=pltpu.CompilerParams(vmem_limit_bytes=16 * 1024 * 1024),
+        compiler_params=pltpu.CompilerParams(vmem_limit_bytes=56 * 1024 * 1024),
         cost_estimate=pl.CostEstimate(flops=0, bytes_accessed=5_000_000, transcendentals=0),
     )(full, grads)
     out_field = out.reshape(SLAB, CY, CZ, LANES)

time: 65.1 us -> 68.5 us (1.052)
  Pallas kernels: 60.2 us -> 67.5 us
  local copies, waits for them, and re-layouts: 4.02 us -> 0 us
    pallas_call x1, Pallas kernels: 3.1 us -> 17.3 us  [shards(): pl.pallas_call(finish, out_shape=(jax.ShapeDtypeStruct((SLAB * CELLS, LAN...]
    pallas_call x1, Pallas kernels: 57.1 us -> 50.2 us  [shards(): pl.pallas_call(kernel, out_shape=(jax.ShapeDtypeStruct((AF_TOTAL, LANES),...]
    unnamed x8 -> x0, local copies, waits for them, and re-layouts: 4.02 us -> none
where the time goes in v1:
time: 68.5 us; the launch traced here: 68.3 us
  Pallas kernels  67.5 us (99%)
  between operations  0.8 us (1%)
    pallas_call x1, Pallas kernels, shards(): pl.pallas_call(kernel, out_shape=(jax.ShapeDtypeStruct((AF_TOTAL, LANES),...  50.2 us
    pallas_call x1, Pallas kernels, shards(): pl.pallas_call(finish, out_shape=(jax.ShapeDtypeStruct((SLAB * CELLS, LAN...  17.3 us

profile of v1, /device:TPU:1, one launch (start us, length us, event | category | flops | bytes accessed | tf_op | source)
XLA Modules:
  0.0 68.3 jit_solution(16722195028124887192)
XLA Ops:
  0.6 50.2 %shard_map.75 = (bf16[5120,128]{1,0:T(8,128)(2,1)}, bf16[1792,128]{1,0:T(8,128)(2,1)}) custom-call(bf16[2880,128]{1,0:T(8,128)(2,1)} %bitcast.16, bf16[4,16,32,128]{3,2,1,0:T(8,128)(2,1)} %cot.1, bf16[9,96,128]{2,1,0:T(8,128)(2,1)} %bitcast.20, bf16[9,96,128]{2,1,0:T(8,128)(2,1)} %bitcast.21), custom_call_target="tpu_custom_call" | custom-call | flops 4000000000 | bytes 8000000 | tf_op jit(solution)/shard_map/pallas_call | solution.py:502
  50.8 17.3 %shard_map.76 = (bf16[2048,128]{1,0:T(8,128)(2,1)}, f32[2880,128]{1,0:T(8,128)}, f32[864,128]{1,0:T(8,128)}, f32[864,128]{1,0:T(8,128)}) custom-call(bf16[5120,128]{1,0:T(8,128)(2,1)} %get-tuple-element.10.full, bf16[1792,128]{1,0:T(8,128)(2,1)} %get-tuple-element.11.grads), custom_call_target="tpu_custom_call" | custom-call | bytes 5000000 | tf_op jit(solution)/shard_map/pallas_call | solution.py:548

commit v2 on v1

--- a/solution.py
+++ b/solution.py
@@ -344,15 +344,6 @@
     out_a, out_b, field_a, field_b, field_c = [AfSum(p) for p in range(5)]
     grads = GxSum()
 
-    lax.fori_loop(0, 2, outer_weights, 0)
-    for acc, base in ((AI, 0), (AO, GRAD)):
-        for a in range(3):
-            for b in range(3):
-                WB[pl.ds(base + (a * 3 + b) * 3 * MID, 3 * MID), :] = acc[
-                    b * LANES : b * LANES + 3 * MID, a * LANES : (a + 1) * LANES
-                ].astype(BF)
-    grads.advance()
-
     def out_plane(slot):
         i = ORDER[slot]
         lhs = jnp.concatenate(
@@ -391,20 +382,6 @@
             base = FIELD_BASE + slot * FIELD_SLOT
             for line in range(CY):
                 EXTRA[pl.ds(base + (line + 2) * FZ + 2, CZ), :] = C[ORDER[slot] + 1, line + 2].astype(F32)
-
-    out_plane(0)
-    out_plane(1)
-    out_a.advance()
-    field_plane(0)
-    out_a.advance()
-    field_plane(1)
-    field_a.advance()
-    lax.fori_loop(0, CY, extra_out, 0)
-    extra_field()
-    field_a.advance()
-
-    for copy in second_halos:
-        copy.wait_recv()
 
     def unpack(i, _):
         packed = QR[i].astype(F32)
@@ -417,6 +394,26 @@
             P3[5 * i, pl.ds(2 + r * HALF, HALF)] = grad.astype(BF)
         return 0
 
+    out_plane(0)
+    out_plane(1)
+    out_a.advance()
+    field_plane(0)
+    field_plane(1)
+    field_a.advance()
+    out_a.advance()
+    lax.fori_loop(0, 2, outer_weights, 0)
+    for acc, base in ((AI, 0), (AO, GRAD)):
+        for a in range(3):
+            for b in range(3):
+                WB[pl.ds(base + (a * 3 + b) * 3 * MID, 3 * MID), :] = acc[
+                    b * LANES : b * LANES + 3 * MID, a * LANES : (a + 1) * LANES
+                ].astype(BF)
+    field_a.advance()
+    grads.advance()
+    lax.fori_loop(0, CY, extra_out, 0)
+    extra_field()
+    for copy in second_halos:
+        copy.wait_recv()
     lax.fori_loop(0, 2, unpack, 0)
     out_plane(2)
     out_plane(3)
@@ -452,7 +449,7 @@
         copy.wait_send()
 
 
-def finish(full, grads, out_ref, field_ref, inner_ref, outer_ref, f_in, g_in, f_out, w_out, in_sem, out_sem):
+def finish(full, grads, out_ref, field_ref, inner_ref, outer_ref, f_in, g_in, o_in, f_out, w_out, in_sem, out_sem):
     lines = 4
     steps = FY // lines
     rows = lines * FZ
@@ -465,10 +462,12 @@
 
     inputs = [[source(step, slot) for slot in range(SLAB)] for step in range(steps)]
     whole = pltpu.make_async_copy(grads, g_in, in_sem.at[steps, 0])
+    planes = pltpu.make_async_copy(full.at[pl.ds(0, SLAB * CELLS)], o_in, in_sem.at[steps, 1])
     for copies in inputs:
         for copy in copies:
             copy.start()
     whole.start()
+    planes.start()
     stores = []
 
     def store(src, dst):
@@ -476,8 +475,6 @@
         copy.start()
         stores.append(copy)
 
-    for slot in range(SLAB):
-        store(full.at[pl.ds(slot * CELLS, CELLS)], out_ref.at[pl.ds(ORDER[slot] * CELLS, CELLS)])
     for step in range(steps):
         for slot in range(SLAB):
             inputs[step][slot].wait()
@@ -489,6 +486,9 @@
         part = pl.ds(p * GRAD, GRAD)
         w_out[part, :] = g_in[part, :].astype(F32)
         store(w_out.at[part], ref)
+    planes.wait()
+    for slot in range(SLAB):
+        store(o_in.at[pl.ds(slot * CELLS, CELLS)], out_ref.at[pl.ds(ORDER[slot] * CELLS, CELLS)])
     for copy in stores:
         copy.wait()
 
@@ -558,6 +558,7 @@
         scratch_shapes=[
             pltpu.VMEM((5, SLAB, 4 * FZ, LANES), BF),
             pltpu.VMEM((W_ROWS, LANES), BF),
+            pltpu.VMEM((SLAB * CELLS, LANES), BF),
             pltpu.VMEM((SLAB * PLANE, LANES), F32),
             pltpu.VMEM((2 * GRAD, LANES), F32),
             dma((6, SLAB)), dma((11,)),

time: 68.5 us -> 52.2 us (0.76)
  Pallas kernels: 67.5 us -> 51.2 us
    pallas_call x1, Pallas kernels: 17.3 us -> 2.79 us  [shards(): pl.pallas_call(finish, out_shape=(jax.ShapeDtypeStruct((SLAB * CELLS, LAN...]
    pallas_call x1, Pallas kernels: 50.2 us -> 48.4 us  [shards(): pl.pallas_call(kernel, out_shape=(jax.ShapeDtypeStruct((AF_TOTAL, LANES),...]
where the time goes in v2:
time: 52.2 us; the launch traced here: 52 us
  Pallas kernels  51.2 us (98%)
  between operations  0.8 us (2%)
    pallas_call x1, Pallas kernels, shards(): pl.pallas_call(kernel, out_shape=(jax.ShapeDtypeStruct((AF_TOTAL, LANES),...  48.4 us
    pallas_call x1, Pallas kernels, shards(): pl.pallas_call(finish, out_shape=(jax.ShapeDtypeStruct((SLAB * CELLS, LAN...  2.79 us

profile of v2, /device:TPU:1, one launch (start us, length us, event | category | flops | bytes accessed | tf_op | source)
XLA Modules:
  0.0 52.0 jit_solution(8335731240837363717)
XLA Ops:
  0.6 48.4 %shard_map.75 = (bf16[5120,128]{1,0:T(8,128)(2,1)}, bf16[1792,128]{1,0:T(8,128)(2,1)}) custom-call(bf16[2880,128]{1,0:T(8,128)(2,1)} %bitcast.16, bf16[4,16,32,128]{3,2,1,0:T(8,128)(2,1)} %cot.1, bf16[9,96,128]{2,1,0:T(8,128)(2,1)} %bitcast.20, bf16[9,96,128]{2,1,0:T(8,128)(2,1)} %bitcast.21), custom_call_target="tpu_custom_call" | custom-call | flops 4000000000 | bytes 8000000 | tf_op jit(solution)/shard_map/pallas_call | solution.py:502
  49.1 2.8 %shard_map.76 = (bf16[2048,128]{1,0:T(8,128)(2,1)}, f32[2880,128]{1,0:T(8,128)}, f32[864,128]{1,0:T(8,128)}, f32[864,128]{1,0:T(8,128)}) custom-call(bf16[5120,128]{1,0:T(8,128)(2,1)} %get-tuple-element.10.full, bf16[1792,128]{1,0:T(8,128)(2,1)} %get-tuple-element.11.grads), custom_call_target="tpu_custom_call" | custom-call | bytes 5000000 | tf_op jit(solution)/shard_map/pallas_call | solution.py:548

commit v3 on v2

v3 whole, which is shorter than its diff:
```python
import jax
import jax.numpy as jnp
from jax import lax
from jax.experimental import pallas as pl
from jax.experimental.pallas import tpu as pltpu
from jax.sharding import PartitionSpec as P

MESH = pl.DeviceIdType.MESH
BF = jnp.bfloat16
F32 = jnp.float32

SLAB = 4
CY, CZ = 16, 32
PITCH = 48
LANES = 128
MID = 32
TWO = 2 * MID
FY, FZ = 20, 36
HY, DY, OY, GY = 10, 12, 8, 10
DROWS = DY * FZ
BLOCKS = 5
ORDER = (1, 2, 0, 3)

OUT_SLOT = OY * CZ
FIELD_SLOT = 384
FIELD_BASE = SLAB * OUT_SLOT
AF_ROWS = (2 * OUT_SLOT, 2 * OUT_SLOT, 2 * FIELD_SLOT, FIELD_SLOT, FIELD_SLOT)
AF_BASE = tuple(sum(AF_ROWS[:p]) for p in range(5))
AF_TOTAL = sum(AF_ROWS)
AF_LAND = tuple(7 * base // 8 for base in AF_BASE)
GRAD = 27 * MID
W_ROWS = 1792
W_PART = W_ROWS // 4


def align(value, by=16):
    return pl.multiple_of(value, by)


def kernel(
    disp, cot, win, wout,
    full_ref, grads_ref,
    raw, D, C, HA, HB, PA, PB, WIN, WOUT, W1T, W1, W2T, W2, AI, AO, DF, FS, EXTRA, B, R, WB, WZ, WR, QS, QR, HS, HL, HF,
    land_af, land_wc, land_z, land_x,
    load_sem, halo_s, halo_r, core_s, core_r, rs_s, rs_r, ag_s, ag_r, ws_s, ws_r, wx_s, wx_r, wg_s, wg_r, store_sem,
):
    gx = lax.axis_index("gx")
    af = lax.axis_index("af")
    core = lax.rem(af, 2)
    y = lax.rem(lax.div(af, 2), 4)
    xl = lax.div(af, 8)
    z = lax.rem(gx, 4)
    xh = lax.div(gx, 4)

    af_peers, z_peers = [], []
    for dx, dy in ((1, 2), (0, 2), (1, 1), (1, 3), (0, 1), (0, 3), (1, 0)):
        x2, y2 = lax.rem(xl + dx, 2), lax.rem(y + dy, 4)
        af_peers.append(((gx, (x2 * 4 + y2) * 2 + core), x2 * 4 + y2))
    for dz in (2, 1, 3):
        z2 = lax.rem(z + dz, 4)
        z_peers.append(((xh * 4 + z2, af), z2))
    x_peer = ((1 - xh) * 4 + z, af)
    other_core = (gx, af + 1 - 2 * core)
    right = (lax.rem(gx + 1, 8), af)
    left = (lax.rem(gx + 7, 8), af)

    cot_lines = pl.ds(2 - 2 * core, HY)
    loads = [
        pltpu.make_async_copy(disp.at[pl.ds(align(core * 8 * FZ * SLAB), DY * FZ * SLAB)], raw, load_sem.at[0]),
        pltpu.make_async_copy(cot.at[:, pl.ds(6 * core, HY)], C.at[pl.ds(1, SLAB), cot_lines], load_sem.at[1]),
        pltpu.make_async_copy(win, WIN.at[core], load_sem.at[2]),
        pltpu.make_async_copy(wout, WOUT.at[core], load_sem.at[3]),
    ]
    for load in loads:
        load.start()
    barrier = pltpu.get_barrier_semaphore()
    peers = [peer for peer, _ in af_peers + z_peers] + [x_peer, other_core, left, right]
    for peer in peers:
        pl.semaphore_signal(barrier, inc=1, device_id=peer, device_id_type=MESH)

    C[:, pl.ds(10 * core, 2)] = jnp.zeros((6, 2, CZ, LANES), BF)
    PA[:, pl.ds(10 * core, 2)] = jnp.zeros((6, 2, PITCH, LANES), BF)
    PB[:, pl.ds(10 * core + 1, 2)] = jnp.zeros((6, 2, PITCH, LANES), BF)
    DF[DROWS * SLAB:, :] = jnp.zeros((SLAB * (PITCH - FZ), LANES), F32)
    HF[DROWS:, :] = jnp.zeros((16, LANES), F32)
    for straight in (W1, W2):
        for a in range(3):
            straight[pl.ds((a * BLOCKS + 4) * LANES + TWO, TWO), :] = jnp.zeros((TWO, LANES), BF)
    AI[...] = jnp.zeros_like(AI)
    AO[...] = jnp.zeros_like(AO)
    for k in range(2):
        WB[k, 2 * GRAD:, :] = jnp.zeros((W_ROWS - 2 * GRAD, LANES), BF)
    for slot in range(SLAB):
        FS[pl.ds(slot * FIELD_SLOT + GY * FZ, FIELD_SLOT - GY * FZ), :] = jnp.zeros(
            (FIELD_SLOT - GY * FZ, LANES), F32
        )

    loads[0].wait()
    line_row = lax.broadcasted_iota(jnp.int32, (PITCH, LANES), 0)

    def widen(i, _):
        rows = pl.ds(align(i * 4 * FZ * SLAB), 4 * FZ * SLAB)
        DF[rows, :] = raw[rows, :].astype(F32)
        return 0

    lax.fori_loop(0, DY // 4, widen, 0)
    for side, x in enumerate((0, SLAB - 1)):
        HS[side] = DF[pl.ds(x, DROWS, stride=SLAB), :].astype(BF)

    def part(i, _):
        for x in range(SLAB):
            line = DF[pl.ds(i * FZ * SLAB + x, PITCH, stride=SLAB), :]
            D[x + 1, i] = jnp.where(line_row < FZ, line, 0.0).astype(BF)
        return 0

    lax.fori_loop(0, DY, part, 0)
    for load in loads[1:]:
        load.wait()

    def halo(index, src, dst, peer):
        copy = pltpu.make_async_remote_copy(
            src_ref=src, dst_ref=dst, send_sem=halo_s.at[index], recv_sem=halo_r.at[index],
            device_id=peer, device_id_type=MESH,
        )
        copy.start()
        halos.append(copy)
        return copy

    halos = []
    pl.semaphore_wait(barrier, len(peers))
    weights = [
        halo(0, WIN.at[core], WIN.at[core], other_core),
        halo(1, WOUT.at[core], WOUT.at[core], other_core),
    ]
    first_halos = [
        halo(2, HS.at[1], HL.at[0], right),
        halo(3, HS.at[0], HL.at[1], left),
        halo(4, C.at[SLAB, cot_lines], C.at[0, cot_lines], right),
        halo(5, C.at[1, cot_lines], C.at[SLAB + 1, cot_lines], left),
    ]

    def extra_out(i, _):
        for slot in range(SLAB):
            EXTRA[pl.ds(align(slot * OUT_SLOT + i * CZ), CZ), :] = DF[
                pl.ds((i + 2) * FZ * SLAB + 2 * SLAB + ORDER[slot], CZ, stride=SLAB), :
            ]
        return 0

    lax.fori_loop(0, OY, extra_out, 0)
    EXTRA[FIELD_BASE:, :] = jnp.zeros((SLAB * FIELD_SLOT, LANES), F32)
    for slot in range(SLAB):
        base = FIELD_BASE + slot * FIELD_SLOT
        for line in range(GY):
            EXTRA[pl.ds(base + line * FZ + 2, CZ), :] = C[ORDER[slot] + 1, 2 * core + line].astype(F32)

    for copy in weights:
        copy.wait_recv()

    def places(blocks_c2):
        table = {(b, c): b * LANES + c * TWO for b in range(3) for c in range(2)}
        for b, row in enumerate(blocks_c2):
            table[b, 2] = row
        return table

    in_places = places((4 * LANES, 3 * LANES + TWO, 3 * LANES))
    out_places = places((3 * LANES, 3 * LANES + TWO, 4 * LANES))
    for src, straight, turned, table in ((WIN, W1, W1T, in_places), (WOUT, W2, W2T, out_places)):
        for a in range(3):
            for (b, c), row in table.items():
                for k in range(2):
                    straight[pl.ds(a * BLOCKS * LANES + row + k * MID, MID), :] = src[
                        k, pl.ds(((a * 3 + b) * 3 + c) * MID, MID), :
                    ]
        for a in range(3):
            for b in range(3):
                rows = pl.ds((a * 3 + b) * LANES, LANES)
                turned[rows, :LANES] = straight[pl.ds((a * BLOCKS + b) * LANES, LANES), :].T
                row = table[b, 2]
                pair = straight[pl.ds(a * BLOCKS * LANES + row // LANES * LANES, LANES), :]
                if row % LANES:
                    pair = jnp.concatenate([pair[TWO:], pair[:TWO]], axis=0)
                turned[rows, LANES:] = pair.T

    def lane_half(values):
        return pltpu.roll(values, TWO, 1)

    def row_roll(values, count):
        return pltpu.roll(values, count % values.shape[0], 0)

    def gather(values, direction):
        near, far = values[:, :LANES], values[:, LANES:]
        return near + row_roll(lane_half(near), -direction) + row_roll(far, -2 * direction)

    def first_mids(values):
        lane = lax.broadcasted_iota(jnp.int32, values.shape, 1)
        return jnp.where(lane < TWO, values, 0.0)

    rows = HY * PITCH

    def store_hidden(plane, hidden):
        near = hidden + lane_half(row_roll(hidden, -1))
        far = row_roll(hidden, -2).reshape(HY, PITCH, LANES)[:, :CZ].reshape(HY * CZ, LANES)
        later = jnp.concatenate([far[CZ:], jnp.zeros((CZ, LANES), F32)], axis=0)
        HA[plane] = near.reshape(HY, PITCH, LANES)[:, :CZ].astype(BF)
        HB[plane] = (far + lane_half(later)).reshape(HY, CZ, LANES).astype(BF)

    def store_grad(plane, grad):
        near = grad + lane_half(row_roll(grad, 1))
        far = row_roll(grad, 2)
        nothing = jnp.zeros((PITCH, LANES), F32)
        both = jnp.concatenate([nothing, far], axis=0) + lane_half(jnp.concatenate([far, nothing], axis=0))
        PA[plane, pl.ds(2 - 2 * core, HY)] = near.reshape(HY, PITCH, LANES).astype(BF)
        PB[plane, pl.ds(2 - 2 * core, HY + 1)] = both.reshape(HY + 1, PITCH, LANES).astype(BF)

    def stage_one(x):
        lhs = jnp.concatenate(
            [D[x + a, pl.ds(b, HY)].reshape(rows, LANES) for a in range(3) for b in range(3)], axis=1
        )
        pre = gather(jnp.dot(lhs, W1T[...], preferred_element_type=F32), 1)
        lhs = jnp.concatenate(
            [
                C[x + 2 - a, pl.ds(2 - b, HY)].reshape(HY * CZ, LANES)
                for a in range(3)
                for b in range(3)
            ],
            axis=1,
        )
        back = jnp.dot(lhs, W2T[...], preferred_element_type=F32).reshape(HY, CZ, 2 * LANES)
        back = jnp.concatenate([back, jnp.zeros((HY, PITCH - CZ, 2 * LANES), F32)], axis=1)
        grad = gather(back.reshape(rows, 2 * LANES), -1)
        square = pre * pre + 0.01
        inverse = lax.rsqrt(square)
        hidden = first_mids(0.505 * pre + 0.495 * (square * inverse))
        grad = first_mids(grad * (0.505 + 0.495 * (pre * inverse)))
        store_hidden(x + 1, hidden)
        store_grad(x + 1, grad)
        return hidden, grad

    def outer_plane(i):
        hidden, grad = stage_one(3 * i)
        QS[i] = (hidden + lane_half(grad)).astype(BF)

    over_rows = (((0,), (0,)), ((), ()))

    def hidden_blocks(plane):
        blocks = [HA[plane, pl.ds(b, OY)] for b in range(3)] + [HB[plane, pl.ds(b, OY)] for b in (0, 2)]
        return [block.reshape(OUT_SLOT, LANES) for block in blocks]

    def grad_blocks(plane):
        blocks = [PA[plane, pl.ds(2 - b, GY)] for b in range(3)] + [PB[plane, pl.ds(b, GY)] for b in (1, 3)]
        return [block.reshape(GY * PITCH, LANES) for block in blocks]

    def weight_terms(i):
        right_side = jnp.concatenate(
            [C[i + 2 - a, pl.ds(2, OY)].reshape(OUT_SLOT, LANES) for a in range(3)], axis=1
        )
        AO[...] += lax.dot_general(
            jnp.concatenate(hidden_blocks(i + 1), axis=1), right_side, over_rows, preferred_element_type=F32
        )
        right_side = jnp.concatenate(
            [D[i + a, pl.ds(2 * core, GY)].reshape(GY * PITCH, LANES) for a in range(3)], axis=1
        )
        AI[...] += lax.dot_general(
            jnp.concatenate(grad_blocks(i + 1), axis=1), right_side, over_rows, preferred_element_type=F32
        )

    def inner_weights(i, _):
        weight_terms(1 + i)
        return 0

    def outer_weights(i, _):
        weight_terms(3 * i)
        return 0

    stage_one(1)
    stage_one(2)
    lax.fori_loop(0, 2, inner_weights, 0)
    for side in range(2):
        first_halos[side].wait_recv()
        HF[0:DROWS, :] = HL[side].astype(F32)
        for line in range(DY):
            value = HF[pl.ds(line * FZ, PITCH), :]
            D[side * (SLAB + 1), line] = jnp.where(line_row < FZ, value, 0.0).astype(BF)
    for side in range(2):
        first_halos[2 + side].wait_recv()
    outer_plane(0)
    second_halos = [halo(6, QS.at[0], QR.at[1], left)]
    outer_plane(1)
    second_halos.append(halo(7, QS.at[1], QR.at[0], right))

    sends = []

    def send(src, dst, send_sem, recv_sem, peer):
        copy = pltpu.make_async_remote_copy(
            src_ref=src, dst_ref=dst, send_sem=send_sem, recv_sem=recv_sem, device_id=peer, device_id_type=MESH
        )
        copy.start()
        sends.append(copy)
        return copy

    def scatter(peers, piece, landing, size, sems):
        return [
            send(piece(align(place * size), size), landing(j), sems[0](j), sems[1](j), peer)
            for j, (peer, place) in enumerate(peers)
        ]

    def total(copies, piece, landing, me, size):
        for copy in copies:
            copy.wait_recv()
        value = piece(align(me * size), size)[...].astype(F32)
        for j in range(len(copies)):
            value = value + landing(j)[...].astype(F32)
        return value

    def spread_out(peers, whole, me, size, sems):
        rows = whole(align(me * size), size)
        return [send(rows, rows, sems[0](j), sems[1](j), peer) for j, (peer, _) in enumerate(peers)]

    class AfSum:
        def __init__(self, p):
            self.p, self.size = p, AF_ROWS[p] // 8
            self.me = xl * 4 + y
            self.landing = lambda j: land_af.at[pl.ds(AF_LAND[p] + j * self.size, self.size)]
            self.step = 0

        def piece(self, off, size):
            return B.at[pl.ds(align(AF_BASE[self.p] + off), size)]

        def whole(self, off, size):
            return R.at[core, pl.ds(align(AF_BASE[self.p] + off), size)]

        def advance(self):
            p, me, size = self.p, self.me, self.size
            if self.step == 0:
                sems = (lambda j: rs_s.at[p, j], lambda j: rs_r.at[p, j])
                self.copies = scatter(af_peers, self.piece, self.landing, size, sems)
            elif self.step == 1:
                value = total(self.copies, self.piece, self.landing, me, size)
                value = value + EXTRA[pl.ds(align(AF_BASE[p] + me * size), size), :]
                self.whole(align(me * size), size)[...] = value.astype(BF)
                sems = (lambda j: ag_s.at[p, j], lambda j: ag_r.at[p, j])
                self.copies = spread_out(af_peers, self.whole, me, size, sems)
            elif self.step == 2:
                for copy in self.copies:
                    copy.wait_recv()
                rows = self.whole(0, AF_ROWS[p])
                self.copies = [send(rows, rows, core_s.at[p], core_r.at[p], other_core)]
            else:
                self.copies[0].wait_recv()
                rows = pl.ds(AF_BASE[p], AF_ROWS[p])
                store = pltpu.make_async_copy(R.at[:, rows], full_ref.at[:, rows], store_sem.at[p])
                store.start()
                stores.append(store)
            self.step += 1

    class GxSum:
        def __init__(self):
            self.step = 0

        def piece(self, off, size):
            return WB.at[core, pl.ds(off, size)]

        def whole(self, off, size):
            return WR.at[pl.ds(off, size)]

        def advance(self):
            if self.step == 0:
                self.copies = [send(WB.at[1 - core], land_wc, core_s.at[5], core_r.at[5], other_core)]
            elif self.step == 1:
                self.copies[0].wait_recv()
                mine = WB.at[core]
                mine[...] = (mine[...].astype(F32) + land_wc[...].astype(F32)).astype(BF)
                sems = (lambda j: ws_s.at[j], lambda j: ws_r.at[j])
                self.copies = scatter(z_peers, self.piece, lambda j: land_z.at[j], W_PART, sems)
            elif self.step == 2:
                WZ[...] = total(self.copies, self.piece, lambda j: land_z.at[j], z, W_PART).astype(BF)
                self.copies = [send(WZ, land_x, wx_s.at[0], wx_r.at[0], x_peer)]
            elif self.step == 3:
                self.copies[0].wait_recv()
                value = WZ[...].astype(F32) + land_x[...].astype(F32)
                self.whole(align(z * W_PART), W_PART)[...] = value.astype(BF)
                sems = (lambda j: wg_s.at[j], lambda j: wg_r.at[j])
                self.copies = spread_out(z_peers, self.whole, z, W_PART, sems)
            else:
                for copy in self.copies:
                    copy.wait_recv()
                store = pltpu.make_async_copy(WR, grads_ref, store_sem.at[5])
                store.start()
                stores.append(store)
            self.step += 1

    stores = []
    out_a, out_b, field_a, field_b, field_c = [AfSum(p) for p in range(5)]
    grads = GxSum()

    def out_plane(slot):
        i = ORDER[slot]
        lhs = jnp.concatenate([block for a in range(3) for block in hidden_blocks(i + a)], axis=1)
        B[pl.ds(slot * OUT_SLOT, OUT_SLOT), :] = jnp.dot(lhs, W2[...], preferred_element_type=F32).astype(BF)

    def field_plane(slot):
        i = ORDER[slot]
        lhs = jnp.concatenate([block for a in range(3) for block in grad_blocks(i + 2 - a)], axis=1)
        block = jnp.dot(lhs, W1[...], preferred_element_type=F32).reshape(GY, PITCH, LANES)
        base = slot * FIELD_SLOT
        for line in range(GY):
            FS[pl.ds(base + line * FZ, FZ), :] = block[line, :FZ]
        B[pl.ds(FIELD_BASE + base, FIELD_SLOT), :] = FS[pl.ds(base, FIELD_SLOT), :].astype(BF)

    def edge_weights():
        lax.fori_loop(0, 2, outer_weights, 0)
        for acc, table, base in ((AI, in_places, 0), (AO, out_places, GRAD)):
            for a in range(3):
                for (b, c), row in table.items():
                    for k in range(2):
                        WB[k, pl.ds(base + ((a * 3 + b) * 3 + c) * MID, MID), :] = acc[
                            pl.ds(row + k * MID, MID), a * LANES : (a + 1) * LANES
                        ].astype(BF)

    def neighbours_planes():
        for copy in second_halos:
            copy.wait_recv()
        for side in range(2):
            packed = QR[side].astype(F32)
            store_hidden(5 * side, first_mids(packed))
            store_grad(5 * side, first_mids(lane_half(packed)))

    out_plane(0)
    out_plane(1)
    out_a.advance()
    field_plane(0)
    field_plane(1)
    field_a.advance()
    edge_weights()
    grads.advance()
    neighbours_planes()
    out_plane(2)
    out_plane(3)
    out_b.advance()
    field_plane(2)
    field_b.advance()
    field_plane(3)
    field_c.advance()
    grads.advance()
    out_a.advance()
    field_a.advance()
    out_b.advance()
    grads.advance()
    field_b.advance()
    field_c.advance()
    out_a.advance()
    field_a.advance()
    grads.advance()
    out_b.advance()
    out_a.advance()
    field_a.advance()
    field_b.advance()
    out_b.advance()
    field_c.advance()
    grads.advance()
    field_b.advance()
    field_c.advance()
    for store in stores:
        store.wait()
    for copy in halos + sends:
        copy.wait_send()


def finish(full, grads, out_ref, field_ref, inner_ref, outer_ref, f_in, g_in, o_in, f_out, w_out, in_sem, out_sem):
    inputs = [
        pltpu.make_async_copy(
            full.at[core, pl.ds(FIELD_BASE, SLAB * FIELD_SLOT)], f_in.at[core], in_sem.at[core]
        )
        for core in range(2)
    ]
    whole = pltpu.make_async_copy(grads, g_in, in_sem.at[2])
    planes = pltpu.make_async_copy(full.at[:, pl.ds(0, FIELD_BASE)], o_in, in_sem.at[3])
    for copy in inputs + [whole, planes]:
        copy.start()
    stores = []

    def store(src, dst):
        copy = pltpu.make_async_copy(src, dst, out_sem.at[len(stores)])
        copy.start()
        stores.append(copy)

    rows = GY * FZ
    for core in range(2):
        inputs[core].wait()
        for slot in range(SLAB):
            f_out[pl.ds(core * rows * SLAB + ORDER[slot], rows, stride=SLAB), :] = f_in[
                core, pl.ds(slot * FIELD_SLOT, rows), :
            ].astype(F32)
        part = pl.ds(core * rows * SLAB, rows * SLAB)
        store(f_out.at[part], field_ref.at[part])
    whole.wait()
    for p, ref in enumerate((inner_ref, outer_ref)):
        part = pl.ds(p * GRAD, GRAD)
        w_out[part, :] = g_in[part, :].astype(F32)
        store(w_out.at[part], ref)
    planes.wait()
    for slot in range(SLAB):
        for core in range(2):
            store(
                o_in.at[core, pl.ds(slot * OUT_SLOT, OUT_SLOT)],
                out_ref.at[pl.ds((2 * ORDER[slot] + core) * OUT_SLOT, OUT_SLOT)],
            )
    for copy in stores:
        copy.wait()


def shards(displace, weight_in, weight_out, cotangent):
    hbm = pl.BlockSpec(memory_space=pl.ANY)
    rows = jnp.transpose(displace, (1, 2, 0, 3)).reshape(SLAB * FY * FZ, LANES)
    win = jnp.transpose(weight_in, (0, 1, 2, 4, 3)).reshape(GRAD, LANES)
    wout = weight_out.reshape(GRAD, LANES)
    dma = pltpu.SemaphoreType.DMA
    full, grads = pl.pallas_call(
        kernel,
        out_shape=(
            jax.ShapeDtypeStruct((2, AF_TOTAL, LANES), BF),
            jax.ShapeDtypeStruct((W_ROWS, LANES), BF),
        ),
        in_specs=[hbm] * 4,
        out_specs=[hbm] * 2,
        scratch_shapes=[
            pltpu.VMEM((SLAB * DROWS, LANES), BF),
            pltpu.VMEM((SLAB + 2, DY, PITCH, LANES), BF),
            pltpu.VMEM((SLAB + 2, DY, CZ, LANES), BF),
            pltpu.VMEM((SLAB + 2, HY, CZ, LANES), BF),
            pltpu.VMEM((SLAB + 2, HY, CZ, LANES), BF),
            pltpu.VMEM((SLAB + 2, HY + 2, PITCH, LANES), BF),
            pltpu.VMEM((SLAB + 2, HY + 3, PITCH, LANES), BF),
            pltpu.VMEM((2, GRAD, LANES), BF),
            pltpu.VMEM((2, GRAD, LANES), BF),
            pltpu.VMEM((9 * LANES, 2 * LANES), BF),
            pltpu.VMEM((3 * BLOCKS * LANES, LANES), BF),
            pltpu.VMEM((9 * LANES, 2 * LANES), BF),
            pltpu.VMEM((3 * BLOCKS * LANES, LANES), BF),
            pltpu.VMEM((BLOCKS * LANES, 3 * LANES), F32),
            pltpu.VMEM((BLOCKS * LANES, 3 * LANES), F32),
            pltpu.VMEM((SLAB * (DROWS + PITCH - FZ), LANES), F32),
            pltpu.VMEM((SLAB * FIELD_SLOT, LANES), F32),
            pltpu.VMEM((AF_TOTAL, LANES), F32),
            pltpu.VMEM((AF_TOTAL, LANES), BF),
            pltpu.VMEM((2, AF_TOTAL, LANES), BF),
            pltpu.VMEM((2, W_ROWS, LANES), BF),
            pltpu.VMEM((W_PART, LANES), BF),
            pltpu.VMEM((W_ROWS, LANES), BF),
            pltpu.VMEM((2, HY * PITCH, LANES), BF),
            pltpu.VMEM((2, HY * PITCH, LANES), BF),
            pltpu.VMEM((2, DROWS, LANES), BF),
            pltpu.VMEM((2, DROWS, LANES), BF),
            pltpu.VMEM((DROWS + 16, LANES), F32),
            pltpu.VMEM((7 * AF_TOTAL // 8, LANES), BF),
            pltpu.VMEM((W_ROWS, LANES), BF),
            pltpu.VMEM((3, W_PART, LANES), BF),
            pltpu.VMEM((W_PART, LANES), BF),
            dma((4,)), dma((8,)), dma((8,)),
            dma((6,)), dma((6,)), dma((5, 7)), dma((5, 7)), dma((5, 7)), dma((5, 7)),
            dma((3,)), dma((3,)), dma((1,)), dma((1,)), dma((3,)), dma((3,)), dma((6,)),
        ],
        compiler_params=pltpu.CompilerParams(
            collective_id=0, has_side_effects=True, vmem_limit_bytes=56 * 1024 * 1024
        ),
        cost_estimate=pl.CostEstimate(flops=4_000_000_000, bytes_accessed=8_000_000, transcendentals=400_000),
    )(rows, cotangent, win, wout)
    out, field, inner, outer = pl.pallas_call(
        finish,
        out_shape=(
            jax.ShapeDtypeStruct((SLAB * CY * CZ, LANES), BF),
            jax.ShapeDtypeStruct((SLAB * FY * FZ, LANES), F32),
            jax.ShapeDtypeStruct((GRAD, LANES), F32),
            jax.ShapeDtypeStruct((GRAD, LANES), F32),
        ),
        in_specs=[hbm] * 2,
        out_specs=[hbm] * 4,
        scratch_shapes=[
            pltpu.VMEM((2, SLAB * FIELD_SLOT, LANES), BF),
            pltpu.VMEM((W_ROWS, LANES), BF),
            pltpu.VMEM((2, FIELD_BASE, LANES), BF),
            pltpu.VMEM((SLAB * FY * FZ, LANES), F32),
            pltpu.VMEM((2 * GRAD, LANES), F32),
            dma((4,)), dma((12,)),
        ],
        compiler_params=pltpu.CompilerParams(vmem_limit_bytes=56 * 1024 * 1024),
        cost_estimate=pl.CostEstimate(flops=0, bytes_accessed=5_000_000, transcendentals=0),
    )(full, grads)
    out_field = out.reshape(SLAB, CY, CZ, LANES)
    field_grad = jnp.transpose(field.reshape(FY, FZ, SLAB, LANES), (2, 0, 1, 3))
    inner_grad = jnp.transpose(inner.reshape(3, 3, 3, MID, LANES), (0, 1, 2, 4, 3))
    outer_grad = outer.reshape(3, 3, 3, MID, LANES)
    return (out_field, field_grad, inner_grad, outer_grad)


def solution(mesh):
    return jax.shard_map(
        shards,
        mesh=mesh,
        in_specs=(
            P("gx", None, None, None),
            P(None, None, None, None, "af"),
            P(None, None, None, "af", None),
            P("gx", None, None, None),
        ),
        out_specs=(
            P("gx", None, None, None),
            P("gx", None, None, None),
            P(None, None, None, None, "af"),
            P(None, None, None, "af", None),
        ),
        check_vma=False,
    )
```

time: 52.2 us -> 48.3 us (0.925)
  the two profiles are of different devices: /device:TPU:1 before, /device:TPU:0 now
where the time goes in v3:
time: 48.3 us; the launch traced here: 48.1 us
  Pallas kernels  47.5 us (98%)
  between operations  0.64 us (1%)
    pallas_call x1, Pallas kernels, shards(): pl.pallas_call(kernel, out_shape=(jax.ShapeDtypeStruct((2, AF_TOTAL, LANE...  44.7 us
    pallas_call x1, Pallas kernels, shards(): pl.pallas_call(finish, out_shape=(jax.ShapeDtypeStruct((SLAB * CY * CZ, L...  2.78 us

profile of v3, /device:TPU:0, one launch (start us, length us, event | category | flops | bytes accessed | tf_op | source)
XLA Modules:
  0.0 48.1 jit_solution(10542237294210119131)
XLA Ops:
  0.6 44.7 %shard_map.75 = (bf16[2,2560,128]{2,1,0:T(8,128)(2,1)}, bf16[1792,128]{1,0:T(8,128)(2,1)}) custom-call(bf16[2880,128]{1,0:T(8,128)(2,1)} %bitcast.16, bf16[4,16,32,128]{3,2,1,0:T(8,128)(2,1)} %cot.1, bf16[864,128]{1,0:T(8,128)(2,1)} %bitcast.20, bf16[864,128]{1,0:T(8,128)(2,1)} %bitcast.21), custom_call_target="tpu_custom_call" | custom-call | flops 4000000000 | bytes 8000000 | tf_op jit(solution)/shard_map/pallas_call | solution.py:518
  45.3 2.8 %shard_map.76 = (bf16[2048,128]{1,0:T(8,128)(2,1)}, f32[2880,128]{1,0:T(8,128)}, f32[864,128]{1,0:T(8,128)}, f32[864,128]{1,0:T(8,128)}) custom-call(bf16[2,2560,128]{2,1,0:T(8,128)(2,1)} %get-tuple-element.10.full, bf16[1792,128]{1,0:T(8,128)(2,1)} %get-tuple-element.11.grads), custom_call_target="tpu_custom_call" | custom-call | bytes 5000000 | tf_op jit(solution)/shard_map/pallas_call | solution.py:568

commit v4 on v3

--- a/solution.py
+++ b/solution.py
@@ -23,14 +23,14 @@
 
 OUT_SLOT = OY * CZ
 FIELD_SLOT = 384
-FIELD_BASE = SLAB * OUT_SLOT
-AF_ROWS = (2 * OUT_SLOT, 2 * OUT_SLOT, 2 * FIELD_SLOT, FIELD_SLOT, FIELD_SLOT)
-AF_BASE = tuple(sum(AF_ROWS[:p]) for p in range(5))
-AF_TOTAL = sum(AF_ROWS)
-AF_LAND = tuple(7 * base // 8 for base in AF_BASE)
+AF_ROWS = 2 * (OUT_SLOT + FIELD_SLOT)
+AF_PIECES = 2
+AF_TOTAL = AF_PIECES * AF_ROWS
+OUT_BASE = tuple(slot // 2 * AF_ROWS + slot % 2 * OUT_SLOT for slot in range(SLAB))
+FIELD_BASE = tuple(slot // 2 * AF_ROWS + 2 * OUT_SLOT + slot % 2 * FIELD_SLOT for slot in range(SLAB))
 GRAD = 27 * MID
-W_ROWS = 1792
-W_PART = W_ROWS // 4
+W_SLOT = 896
+W_PART = W_SLOT // 4
 
 
 def align(value, by=16):
@@ -40,7 +40,7 @@
 def kernel(
     disp, cot, win, wout,
     full_ref, grads_ref,
-    raw, D, C, HA, HB, PA, PB, WIN, WOUT, W1T, W1, W2T, W2, AI, AO, DF, FS, EXTRA, B, R, WB, WZ, WR, QS, QR, HS, HL, HF,
+    raw, D, C, HA, HB, PA, PB, WIN, WOUT, W1T, W1, W2T, W2, AI, AO, DF, FS, EXTRA, B, R, WB, WZ, WC, HS, HL, HF,
     land_af, land_wc, land_z, land_x,
     load_sem, halo_s, halo_r, core_s, core_r, rs_s, rs_r, ag_s, ag_r, ws_s, ws_r, wx_s, wx_r, wg_s, wg_r, store_sem,
 ):
@@ -67,7 +67,7 @@
     cot_lines = pl.ds(2 - 2 * core, HY)
     loads = [
         pltpu.make_async_copy(disp.at[pl.ds(align(core * 8 * FZ * SLAB), DY * FZ * SLAB)], raw, load_sem.at[0]),
-        pltpu.make_async_copy(cot.at[:, pl.ds(6 * core, HY)], C.at[pl.ds(1, SLAB), cot_lines], load_sem.at[1]),
+        pltpu.make_async_copy(cot.at[:, pl.ds(6 * core, HY)], C.at[pl.ds(2, SLAB), cot_lines], load_sem.at[1]),
         pltpu.make_async_copy(win, WIN.at[core], load_sem.at[2]),
         pltpu.make_async_copy(wout, WOUT.at[core], load_sem.at[3]),
     ]
@@ -78,7 +78,7 @@
     for peer in peers:
         pl.semaphore_signal(barrier, inc=1, device_id=peer, device_id_type=MESH)
 
-    C[:, pl.ds(10 * core, 2)] = jnp.zeros((6, 2, CZ, LANES), BF)
+    C[:, pl.ds(10 * core, 2)] = jnp.zeros((8, 2, CZ, LANES), BF)
     PA[:, pl.ds(10 * core, 2)] = jnp.zeros((6, 2, PITCH, LANES), BF)
     PB[:, pl.ds(10 * core + 1, 2)] = jnp.zeros((6, 2, PITCH, LANES), BF)
     DF[DROWS * SLAB:, :] = jnp.zeros((SLAB * (PITCH - FZ), LANES), F32)
@@ -89,7 +89,8 @@
     AI[...] = jnp.zeros_like(AI)
     AO[...] = jnp.zeros_like(AO)
     for k in range(2):
-        WB[k, 2 * GRAD:, :] = jnp.zeros((W_ROWS - 2 * GRAD, LANES), BF)
+        for p in range(2):
+            WB[k, pl.ds(p * W_SLOT + GRAD, W_SLOT - GRAD), :] = jnp.zeros((W_SLOT - GRAD, LANES), BF)
     for slot in range(SLAB):
         FS[pl.ds(slot * FIELD_SLOT + GY * FZ, FIELD_SLOT - GY * FZ), :] = jnp.zeros(
             (FIELD_SLOT - GY * FZ, LANES), F32
@@ -104,13 +105,13 @@
         return 0
 
     lax.fori_loop(0, DY // 4, widen, 0)
-    for side, x in enumerate((0, SLAB - 1)):
-        HS[side] = DF[pl.ds(x, DROWS, stride=SLAB), :].astype(BF)
+    for x in range(SLAB):
+        HS[x] = DF[pl.ds(x, DROWS, stride=SLAB), :].astype(BF)
 
     def part(i, _):
         for x in range(SLAB):
             line = DF[pl.ds(i * FZ * SLAB + x, PITCH, stride=SLAB), :]
-            D[x + 1, i] = jnp.where(line_row < FZ, line, 0.0).astype(BF)
+            D[x + 2, i] = jnp.where(line_row < FZ, line, 0.0).astype(BF)
         return 0
 
     lax.fori_loop(0, DY, part, 0)
@@ -132,26 +133,29 @@
         halo(0, WIN.at[core], WIN.at[core], other_core),
         halo(1, WOUT.at[core], WOUT.at[core], other_core),
     ]
-    first_halos = [
-        halo(2, HS.at[1], HL.at[0], right),
-        halo(3, HS.at[0], HL.at[1], left),
-        halo(4, C.at[SLAB, cot_lines], C.at[0, cot_lines], right),
-        halo(5, C.at[1, cot_lines], C.at[SLAB + 1, cot_lines], left),
-    ]
+    given = ((3, 1, right), (0, 6, left), (2, 0, right), (1, 7, left))
+    first_halos = []
+    for k, (x, place, peer) in enumerate(given):
+        first_halos.append(
+            (
+                halo(2 + 2 * k, HS.at[x], HL.at[k], peer),
+                halo(3 + 2 * k, C.at[x + 2, cot_lines], C.at[place, cot_lines], peer),
+            )
+        )
 
     def extra_out(i, _):
         for slot in range(SLAB):
-            EXTRA[pl.ds(align(slot * OUT_SLOT + i * CZ), CZ), :] = DF[
+            EXTRA[pl.ds(align(OUT_BASE[slot] + i * CZ), CZ), :] = DF[
                 pl.ds((i + 2) * FZ * SLAB + 2 * SLAB + ORDER[slot], CZ, stride=SLAB), :
             ]
         return 0
 
     lax.fori_loop(0, OY, extra_out, 0)
-    EXTRA[FIELD_BASE:, :] = jnp.zeros((SLAB * FIELD_SLOT, LANES), F32)
     for slot in range(SLAB):
-        base = FIELD_BASE + slot * FIELD_SLOT
+        base = FIELD_BASE[slot]
+        EXTRA[pl.ds(base, FIELD_SLOT), :] = jnp.zeros((FIELD_SLOT, LANES), F32)
         for line in range(GY):
-            EXTRA[pl.ds(base + line * FZ + 2, CZ), :] = C[ORDER[slot] + 1, 2 * core + line].astype(F32)
+            EXTRA[pl.ds(base + line * FZ + 2, CZ), :] = C[ORDER[slot] + 2, 2 * core + line].astype(F32)
 
     for copy in weights:
         copy.wait_recv()
@@ -214,12 +218,12 @@
 
     def stage_one(x):
         lhs = jnp.concatenate(
-            [D[x + a, pl.ds(b, HY)].reshape(rows, LANES) for a in range(3) for b in range(3)], axis=1
+            [D[x + 1 + a, pl.ds(b, HY)].reshape(rows, LANES) for a in range(3) for b in range(3)], axis=1
         )
         pre = gather(jnp.dot(lhs, W1T[...], preferred_element_type=F32), 1)
         lhs = jnp.concatenate(
             [
-                C[x + 2 - a, pl.ds(2 - b, HY)].reshape(HY * CZ, LANES)
+                C[x + 3 - a, pl.ds(2 - b, HY)].reshape(HY * CZ, LANES)
                 for a in range(3)
                 for b in range(3)
             ],
@@ -234,11 +238,14 @@
         grad = first_mids(grad * (0.505 + 0.495 * (pre * inverse)))
         store_hidden(x + 1, hidden)
         store_grad(x + 1, grad)
-        return hidden, grad
-
-    def outer_plane(i):
-        hidden, grad = stage_one(3 * i)
-        QS[i] = (hidden + lane_half(grad)).astype(BF)
+
+    def arrived(k):
+        first_halos[k][0].wait_recv()
+        HF[0:DROWS, :] = HL[k].astype(F32)
+        for line in range(DY):
+            value = HF[pl.ds(line * FZ, PITCH), :]
+            D[given[k][1], line] = jnp.where(line_row < FZ, value, 0.0).astype(BF)
+        first_halos[k][1].wait_recv()
 
     over_rows = (((0,), (0,)), ((), ()))
 
@@ -250,43 +257,33 @@
         blocks = [PA[plane, pl.ds(2 - b, GY)] for b in range(3)] + [PB[plane, pl.ds(b, GY)] for b in (1, 3)]
         return [block.reshape(GY * PITCH, LANES) for block in blocks]
 
-    def weight_terms(i):
+    def outer_terms(i):
         right_side = jnp.concatenate(
-            [C[i + 2 - a, pl.ds(2, OY)].reshape(OUT_SLOT, LANES) for a in range(3)], axis=1
+            [C[i + 3 - a, pl.ds(2, OY)].reshape(OUT_SLOT, LANES) for a in range(3)], axis=1
         )
         AO[...] += lax.dot_general(
             jnp.concatenate(hidden_blocks(i + 1), axis=1), right_side, over_rows, preferred_element_type=F32
         )
+
+    def inner_terms(i):
         right_side = jnp.concatenate(
-            [D[i + a, pl.ds(2 * core, GY)].reshape(GY * PITCH, LANES) for a in range(3)], axis=1
+            [D[i + 1 + a, pl.ds(2 * core, GY)].reshape(GY * PITCH, LANES) for a in range(3)], axis=1
         )
         AI[...] += lax.dot_general(
             jnp.concatenate(grad_blocks(i + 1), axis=1), right_side, over_rows, preferred_element_type=F32
         )
 
-    def inner_weights(i, _):
-        weight_terms(1 + i)
-        return 0
-
-    def outer_weights(i, _):
-        weight_terms(3 * i)
+    def inner_planes_terms(i, _):
+        outer_terms(1 + i)
+        inner_terms(1 + i)
         return 0
 
     stage_one(1)
     stage_one(2)
-    lax.fori_loop(0, 2, inner_weights, 0)
-    for side in range(2):
-        first_halos[side].wait_recv()
-        HF[0:DROWS, :] = HL[side].astype(F32)
-        for line in range(DY):
-            value = HF[pl.ds(line * FZ, PITCH), :]
-            D[side * (SLAB + 1), line] = jnp.where(line_row < FZ, value, 0.0).astype(BF)
-    for side in range(2):
-        first_halos[2 + side].wait_recv()
-    outer_plane(0)
-    second_halos = [halo(6, QS.at[0], QR.at[1], left)]
-    outer_plane(1)
-    second_halos.append(halo(7, QS.at[1], QR.at[0], right))
+    lax.fori_loop(0, 2, inner_planes_terms, 0)
+    for k, x in ((0, 0), (1, 3)):
+        arrived(k)
+        stage_one(x)
 
     sends = []
 
@@ -316,18 +313,23 @@
         rows = whole(align(me * size), size)
         return [send(rows, rows, sems[0](j), sems[1](j), peer) for j, (peer, _) in enumerate(peers)]
 
+    def keep(src, dst, index):
+        store = pltpu.make_async_copy(src, dst, store_sem.at[index])
+        store.start()
+        stores.append(store)
+
     class AfSum:
         def __init__(self, p):
-            self.p, self.size = p, AF_ROWS[p] // 8
+            self.p, self.size, self.base = p, AF_ROWS // 8, p * AF_ROWS
             self.me = xl * 4 + y
-            self.landing = lambda j: land_af.at[pl.ds(AF_LAND[p] + j * self.size, self.size)]
+            self.landing = lambda j: land_af.at[p, j]
             self.step = 0
 
         def piece(self, off, size):
-            return B.at[pl.ds(align(AF_BASE[self.p] + off), size)]
+            return B.at[pl.ds(align(self.base + off), size)]
 
         def whole(self, off, size):
-            return R.at[core, pl.ds(align(AF_BASE[self.p] + off), size)]
+            return R.at[pl.ds(align(self.base + off), size)]
 
         def advance(self):
             p, me, size = self.p, self.me, self.size
@@ -336,67 +338,67 @@
                 self.copies = scatter(af_peers, self.piece, self.landing, size, sems)
             elif self.step == 1:
                 value = total(self.copies, self.piece, self.landing, me, size)
-                value = value + EXTRA[pl.ds(align(AF_BASE[p] + me * size), size), :]
+                value = value + EXTRA[pl.ds(align(self.base + me * size), size), :]
                 self.whole(align(me * size), size)[...] = value.astype(BF)
                 sems = (lambda j: ag_s.at[p, j], lambda j: ag_r.at[p, j])
                 self.copies = spread_out(af_peers, self.whole, me, size, sems)
             elif self.step == 2:
                 for copy in self.copies:
                     copy.wait_recv()
-                rows = self.whole(0, AF_ROWS[p])
-                self.copies = [send(rows, rows, core_s.at[p], core_r.at[p], other_core)]
+                rows = self.whole(0, AF_ROWS)
+                there = full_ref.at[core, pl.ds(self.base, AF_ROWS)]
+                self.copies = [send(rows, there, core_s.at[p], core_r.at[p], other_core)]
+                keep(rows, there, p)
             else:
                 self.copies[0].wait_recv()
-                rows = pl.ds(AF_BASE[p], AF_ROWS[p])
-                store = pltpu.make_async_copy(R.at[:, rows], full_ref.at[:, rows], store_sem.at[p])
-                store.start()
-                stores.append(store)
             self.step += 1
 
     class GxSum:
-        def __init__(self):
+        def __init__(self, p):
+            self.p, self.base = p, p * W_SLOT
+            self.landing = lambda j: land_z.at[p, j]
             self.step = 0
 
         def piece(self, off, size):
-            return WB.at[core, pl.ds(off, size)]
-
-        def whole(self, off, size):
-            return WR.at[pl.ds(off, size)]
+            return WB.at[core, pl.ds(align(self.base + off), size)]
 
         def advance(self):
+            p, rows = self.p, pl.ds(self.base, W_SLOT)
             if self.step == 0:
-                self.copies = [send(WB.at[1 - core], land_wc, core_s.at[5], core_r.at[5], other_core)]
+                self.copies = [
+                    send(WB.at[1 - core, rows], land_wc.at[p], core_s.at[2 + p], core_r.at[2 + p], other_core)
+                ]
             elif self.step == 1:
                 self.copies[0].wait_recv()
-                mine = WB.at[core]
-                mine[...] = (mine[...].astype(F32) + land_wc[...].astype(F32)).astype(BF)
-                sems = (lambda j: ws_s.at[j], lambda j: ws_r.at[j])
-                self.copies = scatter(z_peers, self.piece, lambda j: land_z.at[j], W_PART, sems)
+                mine = WB.at[core, rows]
+                mine[...] = (mine[...].astype(F32) + land_wc[p].astype(F32)).astype(BF)
+                sems = (lambda j: ws_s.at[p, j], lambda j: ws_r.at[p, j])
+                self.copies = scatter(z_peers, self.piece, self.landing, W_PART, sems)
             elif self.step == 2:
-                WZ[...] = total(self.copies, self.piece, lambda j: land_z.at[j], z, W_PART).astype(BF)
-                self.copies = [send(WZ, land_x, wx_s.at[0], wx_r.at[0], x_peer)]
+                WZ[p] = total(self.copies, self.piece, self.landing, z, W_PART).astype(BF)
+                self.copies = [send(WZ.at[p], land_x.at[p], wx_s.at[p], wx_r.at[p], x_peer)]
             elif self.step == 3:
                 self.copies[0].wait_recv()
-                value = WZ[...].astype(F32) + land_x[...].astype(F32)
-                self.whole(align(z * W_PART), W_PART)[...] = value.astype(BF)
-                sems = (lambda j: wg_s.at[j], lambda j: wg_r.at[j])
-                self.copies = spread_out(z_peers, self.whole, z, W_PART, sems)
+                value = WZ[p].astype(F32) + land_x[p].astype(F32)
+                WC[p] = value.astype(BF)
+                there = grads_ref.at[pl.ds(align(self.base + z * W_PART), W_PART)]
+                self.copies = [
+                    send(WC.at[p], there, wg_s.at[p, j], wg_r.at[p, j], peer) for j, (peer, _) in enumerate(z_peers)
+                ]
+                keep(WC.at[p], there, 2 + p)
             else:
                 for copy in self.copies:
                     copy.wait_recv()
-                store = pltpu.make_async_copy(WR, grads_ref, store_sem.at[5])
-                store.start()
-                stores.append(store)
             self.step += 1
 
     stores = []
-    out_a, out_b, field_a, field_b, field_c = [AfSum(p) for p in range(5)]
-    grads = GxSum()
+    inner_planes, outer_planes = AfSum(0), AfSum(1)
+    inner_sum, outer_sum = GxSum(0), GxSum(1)
 
     def out_plane(slot):
         i = ORDER[slot]
         lhs = jnp.concatenate([block for a in range(3) for block in hidden_blocks(i + a)], axis=1)
-        B[pl.ds(slot * OUT_SLOT, OUT_SLOT), :] = jnp.dot(lhs, W2[...], preferred_element_type=F32).astype(BF)
+        B[pl.ds(OUT_BASE[slot], OUT_SLOT), :] = jnp.dot(lhs, W2[...], preferred_element_type=F32).astype(BF)
 
     def field_plane(slot):
         i = ORDER[slot]
@@ -405,77 +407,70 @@
         base = slot * FIELD_SLOT
         for line in range(GY):
             FS[pl.ds(base + line * FZ, FZ), :] = block[line, :FZ]
-        B[pl.ds(FIELD_BASE + base, FIELD_SLOT), :] = FS[pl.ds(base, FIELD_SLOT), :].astype(BF)
-
-    def edge_weights():
-        lax.fori_loop(0, 2, outer_weights, 0)
-        for acc, table, base in ((AI, in_places, 0), (AO, out_places, GRAD)):
-            for a in range(3):
-                for (b, c), row in table.items():
-                    for k in range(2):
-                        WB[k, pl.ds(base + ((a * 3 + b) * 3 + c) * MID, MID), :] = acc[
-                            pl.ds(row + k * MID, MID), a * LANES : (a + 1) * LANES
-                        ].astype(BF)
-
-    def neighbours_planes():
-        for copy in second_halos:
-            copy.wait_recv()
-        for side in range(2):
-            packed = QR[side].astype(F32)
-            store_hidden(5 * side, first_mids(packed))
-            store_grad(5 * side, first_mids(lane_half(packed)))
-
+        B[pl.ds(FIELD_BASE[slot], FIELD_SLOT), :] = FS[pl.ds(base, FIELD_SLOT), :].astype(BF)
+
+    def collect(acc, table, base):
+        for a in range(3):
+            for (b, c), row in table.items():
+                for k in range(2):
+                    WB[k, pl.ds(base + ((a * 3 + b) * 3 + c) * MID, MID), :] = acc[
+                        pl.ds(row + k * MID, MID), a * LANES : (a + 1) * LANES
+                    ].astype(BF)
+
+    def edge_outer():
+        outer_terms(0)
+        outer_terms(3)
+        collect(AO, out_places, W_SLOT)
+
+    def edge_inner():
+        inner_terms(0)
+        inner_terms(3)
+        collect(AI, in_places, 0)
+
+    def far_planes():
+        for k, x in ((2, -1), (3, 4)):
+            arrived(k)
+            stage_one(x)
+
+    edge_outer()
+    outer_sum.advance()
+    edge_inner()
+    inner_sum.advance()
     out_plane(0)
     out_plane(1)
-    out_a.advance()
     field_plane(0)
     field_plane(1)
-    field_a.advance()
-    edge_weights()
-    grads.advance()
-    neighbours_planes()
+    inner_planes.advance()
+    far_planes()
+    outer_sum.advance()
+    inner_sum.advance()
     out_plane(2)
     out_plane(3)
-    out_b.advance()
     field_plane(2)
-    field_b.advance()
     field_plane(3)
-    field_c.advance()
-    grads.advance()
-    out_a.advance()
-    field_a.advance()
-    out_b.advance()
-    grads.advance()
-    field_b.advance()
-    field_c.advance()
-    out_a.advance()
-    field_a.advance()
-    grads.advance()
-    out_b.advance()
-    out_a.advance()
-    field_a.advance()
-    field_b.advance()
-    out_b.advance()
-    field_c.advance()
-    grads.advance()
-    field_b.advance()
-    field_c.advance()
+    outer_planes.advance()
+    inner_planes.advance()
+    outer_sum.advance()
+    inner_sum.advance()
+    outer_planes.advance()
+    inner_planes.advance()
+    outer_sum.advance()
+    inner_sum.advance()
+    outer_planes.advance()
+    inner_planes.advance()
+    outer_planes.advance()
+    outer_sum.advance()
+    inner_sum.advance()
     for store in stores:
         store.wait()
     for copy in halos + sends:
         copy.wait_send()
 
 
-def finish(full, grads, out_ref, field_ref, inner_ref, outer_ref, f_in, g_in, o_in, f_out, w_out, in_sem, out_sem):
-    inputs = [
-        pltpu.make_async_copy(
-            full.at[core, pl.ds(FIELD_BASE, SLAB * FIELD_SLOT)], f_in.at[core], in_sem.at[core]
-        )
-        for core in range(2)
-    ]
+def finish(full, grads, out_ref, field_ref, inner_ref, outer_ref, f_in, g_in, f_out, w_out, in_sem, out_sem):
+    inputs = [pltpu.make_async_copy(full.at[core], f_in.at[core], in_sem.at[core]) for core in range(2)]
     whole = pltpu.make_async_copy(grads, g_in, in_sem.at[2])
-    planes = pltpu.make_async_copy(full.at[:, pl.ds(0, FIELD_BASE)], o_in, in_sem.at[3])
-    for copy in inputs + [whole, planes]:
+    for copy in inputs + [whole]:
         copy.start()
     stores = []
 
@@ -489,22 +484,20 @@
         inputs[core].wait()
         for slot in range(SLAB):
             f_out[pl.ds(core * rows * SLAB + ORDER[slot], rows, stride=SLAB), :] = f_in[
-                core, pl.ds(slot * FIELD_SLOT, rows), :
+                core, pl.ds(FIELD_BASE[slot], rows), :
             ].astype(F32)
         part = pl.ds(core * rows * SLAB, rows * SLAB)
         store(f_out.at[part], field_ref.at[part])
+        for slot in range(SLAB):
+            store(
+                f_in.at[core, pl.ds(OUT_BASE[slot], OUT_SLOT)],
+                out_ref.at[pl.ds((2 * ORDER[slot] + core) * OUT_SLOT, OUT_SLOT)],
+            )
     whole.wait()
     for p, ref in enumerate((inner_ref, outer_ref)):
         part = pl.ds(p * GRAD, GRAD)
-        w_out[part, :] = g_in[part, :].astype(F32)
+        w_out[part, :] = g_in[pl.ds(p * W_SLOT, GRAD), :].astype(F32)
         store(w_out.at[part], ref)
-    planes.wait()
-    for slot in range(SLAB):
-        for core in range(2):
-            store(
-                o_in.at[core, pl.ds(slot * OUT_SLOT, OUT_SLOT)],
-                out_ref.at[pl.ds((2 * ORDER[slot] + core) * OUT_SLOT, OUT_SLOT)],
-            )
     for copy in stores:
         copy.wait()
 
@@ -519,14 +512,14 @@
         kernel,
         out_shape=(
             jax.ShapeDtypeStruct((2, AF_TOTAL, LANES), BF),
-            jax.ShapeDtypeStruct((W_ROWS, LANES), BF),
+            jax.ShapeDtypeStruct((2 * W_SLOT, LANES), BF),
         ),
         in_specs=[hbm] * 4,
         out_specs=[hbm] * 2,
         scratch_shapes=[
             pltpu.VMEM((SLAB * DROWS, LANES), BF),
-            pltpu.VMEM((SLAB + 2, DY, PITCH, LANES), BF),
-            pltpu.VMEM((SLAB + 2, DY, CZ, LANES), BF),
+            pltpu.VMEM((SLAB + 4, DY, PITCH, LANES), BF),
+            pltpu.VMEM((SLAB + 4, DY, CZ, LANES), BF),
             pltpu.VMEM((SLAB + 2, HY, CZ, LANES), BF),
             pltpu.VMEM((SLAB + 2, HY, CZ, LANES), BF),
             pltpu.VMEM((SLAB + 2, HY + 2, PITCH, LANES), BF),
@@ -543,22 +536,20 @@
             pltpu.VMEM((SLAB * FIELD_SLOT, LANES), F32),
             pltpu.VMEM((AF_TOTAL, LANES), F32),
             pltpu.VMEM((AF_TOTAL, LANES), BF),
-            pltpu.VMEM((2, AF_TOTAL, LANES), BF),
-            pltpu.VMEM((2, W_ROWS, LANES), BF),
-            pltpu.VMEM((W_PART, LANES), BF),
-            pltpu.VMEM((W_ROWS, LANES), BF),
-            pltpu.VMEM((2, HY * PITCH, LANES), BF),
-            pltpu.VMEM((2, HY * PITCH, LANES), BF),
-            pltpu.VMEM((2, DROWS, LANES), BF),
-            pltpu.VMEM((2, DROWS, LANES), BF),
+            pltpu.VMEM((AF_TOTAL, LANES), BF),
+            pltpu.VMEM((2, 2 * W_SLOT, LANES), BF),
+            pltpu.VMEM((2, W_PART, LANES), BF),
+            pltpu.VMEM((2, W_PART, LANES), BF),
+            pltpu.VMEM((SLAB, DROWS, LANES), BF),
+            pltpu.VMEM((SLAB, DROWS, LANES), BF),
             pltpu.VMEM((DROWS + 16, LANES), F32),
-            pltpu.VMEM((7 * AF_TOTAL // 8, LANES), BF),
-            pltpu.VMEM((W_ROWS, LANES), BF),
-            pltpu.VMEM((3, W_PART, LANES), BF),
-            pltpu.VMEM((W_PART, LANES), BF),
-            dma((4,)), dma((8,)), dma((8,)),
-            dma((6,)), dma((6,)), dma((5, 7)), dma((5, 7)), dma((5, 7)), dma((5, 7)),
-            dma((3,)), dma((3,)), dma((1,)), dma((1,)), dma((3,)), dma((3,)), dma((6,)),
+            pltpu.VMEM((AF_PIECES, 7, AF_ROWS // 8, LANES), BF),
+            pltpu.VMEM((2, W_SLOT, LANES), BF),
+            pltpu.VMEM((2, 3, W_PART, LANES), BF),
+            pltpu.VMEM((2, W_PART, LANES), BF),
+            dma((4,)), dma((10,)), dma((10,)),
+            dma((4,)), dma((4,)), dma((2, 7)), dma((2, 7)), dma((2, 7)), dma((2, 7)),
+            dma((2, 3)), dma((2, 3)), dma((2,)), dma((2,)), dma((2, 3)), dma((2, 3)), dma((4,)),
         ],
         compiler_params=pltpu.CompilerParams(
             collective_id=0, has_side_effects=True, vmem_limit_bytes=56 * 1024 * 1024
@@ -576,12 +567,11 @@
         in_specs=[hbm] * 2,
         out_specs=[hbm] * 4,
         scratch_shapes=[
-            pltpu.VMEM((2, SLAB * FIELD_SLOT, LANES), BF),
-            pltpu.VMEM((W_ROWS, LANES), BF),
-            pltpu.VMEM((2, FIELD_BASE, LANES), BF),
+            pltpu.VMEM((2, AF_TOTAL, LANES), BF),
+            pltpu.VMEM((2 * W_SLOT, LANES), BF),
             pltpu.VMEM((SLAB * FY * FZ, LANES), F32),
             pltpu.VMEM((2 * GRAD, LANES), F32),
-            dma((4,)), dma((12,)),
+            dma((3,)), dma((12,)),
         ],
         compiler_params=pltpu.CompilerParams(vmem_limit_bytes=56 * 1024 * 1024),
         cost_estimate=pl.CostEstimate(flops=0, bytes_accessed=5_000_000, transcendentals=0),

time: 48.3 us -> 45.3 us (0.938)
  the two profiles are of different devices: /device:TPU:0 before, /device:TPU:1 now
where the time goes in v4:
time: 45.3 us; the launch traced here: 45.1 us
  Pallas kernels  44.5 us (98%)
  between operations  0.64 us (1%)
    pallas_call x1, Pallas kernels, shards(): pl.pallas_call(kernel, out_shape=(jax.ShapeDtypeStruct((2, AF_TOTAL, LANE...  41.6 us
    pallas_call x1, Pallas kernels, shards(): pl.pallas_call(finish, out_shape=(jax.ShapeDtypeStruct((SLAB * CY * CZ, L...  2.87 us

profile of v4, /device:TPU:1, one launch (start us, length us, event | category | flops | bytes accessed | tf_op | source)
XLA Modules:
  0.0 45.1 jit_solution(9701274699961050166)
XLA Ops:
  0.6 41.6 %shard_map.75 = (bf16[2,2560,128]{2,1,0:T(8,128)(2,1)}, bf16[1792,128]{1,0:T(8,128)(2,1)}) custom-call(bf16[2880,128]{1,0:T(8,128)(2,1)} %bitcast.16, bf16[4,16,32,128]{3,2,1,0:T(8,128)(2,1)} %cot.1, bf16[864,128]{1,0:T(8,128)(2,1)} %bitcast.20, bf16[864,128]{1,0:T(8,128)(2,1)} %bitcast.21), custom_call_target="tpu_custom_call" | custom-call | flops 4000000000 | bytes 8000000 | tf_op jit(solution)/shard_map/pallas_call | solution.py:511
  42.3 2.9 %shard_map.76 = (bf16[2048,128]{1,0:T(8,128)(2,1)}, f32[2880,128]{1,0:T(8,128)}, f32[864,128]{1,0:T(8,128)}, f32[864,128]{1,0:T(8,128)}) custom-call(bf16[2,2560,128]{2,1,0:T(8,128)(2,1)} %get-tuple-element.10.full, bf16[1792,128]{1,0:T(8,128)(2,1)} %get-tuple-element.11.grads), custom_call_target="tpu_custom_call" | custom-call | bytes 5000000 | tf_op jit(solution)/shard_map/pallas_call | solution.py:559

commit v5 on v4

--- a/solution.py
+++ b/solution.py
@@ -23,11 +23,13 @@
 
 OUT_SLOT = OY * CZ
 FIELD_SLOT = 384
-AF_ROWS = 2 * (OUT_SLOT + FIELD_SLOT)
-AF_PIECES = 2
-AF_TOTAL = AF_PIECES * AF_ROWS
-OUT_BASE = tuple(slot // 2 * AF_ROWS + slot % 2 * OUT_SLOT for slot in range(SLAB))
-FIELD_BASE = tuple(slot // 2 * AF_ROWS + 2 * OUT_SLOT + slot % 2 * FIELD_SLOT for slot in range(SLAB))
+PLANE_ROWS = OUT_SLOT + FIELD_SLOT
+AF_ROWS = (2 * PLANE_ROWS, PLANE_ROWS, PLANE_ROWS)
+AF_BASE = (0, 2 * PLANE_ROWS, 3 * PLANE_ROWS)
+AF_TOTAL = SLAB * PLANE_ROWS
+AF_LAND = tuple(7 * base // 8 for base in AF_BASE)
+OUT_BASE = tuple(slot * PLANE_ROWS for slot in range(SLAB))
+FIELD_BASE = tuple(slot * PLANE_ROWS + OUT_SLOT for slot in range(SLAB))
 GRAD = 27 * MID
 W_SLOT = 896
 W_PART = W_SLOT // 4
@@ -320,9 +322,9 @@
 
     class AfSum:
         def __init__(self, p):
-            self.p, self.size, self.base = p, AF_ROWS // 8, p * AF_ROWS
+            self.p, self.rows, self.size, self.base = p, AF_ROWS[p], AF_ROWS[p] // 8, AF_BASE[p]
             self.me = xl * 4 + y
-            self.landing = lambda j: land_af.at[p, j]
+            self.landing = lambda j: land_af.at[pl.ds(AF_LAND[p] + j * self.size, self.size)]
             self.step = 0
 
         def piece(self, off, size):
@@ -345,8 +347,8 @@
             elif self.step == 2:
                 for copy in self.copies:
                     copy.wait_recv()
-                rows = self.whole(0, AF_ROWS)
-                there = full_ref.at[core, pl.ds(self.base, AF_ROWS)]
+                rows = self.whole(0, self.rows)
+                there = full_ref.at[core, pl.ds(self.base, self.rows)]
                 self.copies = [send(rows, there, core_s.at[p], core_r.at[p], other_core)]
                 keep(rows, there, p)
             else:
@@ -366,7 +368,7 @@
             p, rows = self.p, pl.ds(self.base, W_SLOT)
             if self.step == 0:
                 self.copies = [
-                    send(WB.at[1 - core, rows], land_wc.at[p], core_s.at[2 + p], core_r.at[2 + p], other_core)
+                    send(WB.at[1 - core, rows], land_wc.at[p], core_s.at[3 + p], core_r.at[3 + p], other_core)
                 ]
             elif self.step == 1:
                 self.copies[0].wait_recv()
@@ -385,14 +387,14 @@
                 self.copies = [
                     send(WC.at[p], there, wg_s.at[p, j], wg_r.at[p, j], peer) for j, (peer, _) in enumerate(z_peers)
                 ]
-                keep(WC.at[p], there, 2 + p)
+                keep(WC.at[p], there, 3 + p)
             else:
                 for copy in self.copies:
                     copy.wait_recv()
             self.step += 1
 
     stores = []
-    inner_planes, outer_planes = AfSum(0), AfSum(1)
+    inner_planes, low_plane, high_plane = AfSum(0), AfSum(1), AfSum(2)
     inner_sum, outer_sum = GxSum(0), GxSum(1)
 
     def out_plane(slot):
@@ -427,38 +429,42 @@
         inner_terms(3)
         collect(AI, in_places, 0)
 
-    def far_planes():
-        for k, x in ((2, -1), (3, 4)):
-            arrived(k)
-            stage_one(x)
+    def far_plane(k, x):
+        arrived(k)
+        stage_one(x)
 
     edge_outer()
     outer_sum.advance()
-    edge_inner()
-    inner_sum.advance()
     out_plane(0)
     out_plane(1)
     field_plane(0)
     field_plane(1)
     inner_planes.advance()
-    far_planes()
+    edge_inner()
+    inner_sum.advance()
+    far_plane(2, -1)
+    out_plane(2)
+    field_plane(2)
+    low_plane.advance()
     outer_sum.advance()
     inner_sum.advance()
-    out_plane(2)
+    far_plane(3, 4)
     out_plane(3)
-    field_plane(2)
     field_plane(3)
-    outer_planes.advance()
+    high_plane.advance()
     inner_planes.advance()
     outer_sum.advance()
     inner_sum.advance()
-    outer_planes.advance()
+    low_plane.advance()
+    high_plane.advance()
     inner_planes.advance()
     outer_sum.advance()
     inner_sum.advance()
-    outer_planes.advance()
+    low_plane.advance()
+    high_plane.advance()
     inner_planes.advance()
-    outer_planes.advance()
+    low_plane.advance()
+    high_plane.advance()
     outer_sum.advance()
     inner_sum.advance()
     for store in stores:
@@ -468,9 +474,19 @@
 
 
 def finish(full, grads, out_ref, field_ref, inner_ref, outer_ref, f_in, g_in, f_out, w_out, in_sem, out_sem):
-    inputs = [pltpu.make_async_copy(full.at[core], f_in.at[core], in_sem.at[core]) for core in range(2)]
-    whole = pltpu.make_async_copy(grads, g_in, in_sem.at[2])
-    for copy in inputs + [whole]:
+    inputs = [
+        [
+            pltpu.make_async_copy(
+                full.at[core, pl.ds(slot * PLANE_ROWS, PLANE_ROWS)],
+                f_in.at[core, pl.ds(slot * PLANE_ROWS, PLANE_ROWS)],
+                in_sem.at[core, slot],
+            )
+            for slot in range(SLAB)
+        ]
+        for core in range(2)
+    ]
+    whole = pltpu.make_async_copy(grads, g_in, in_sem.at[2, 0])
+    for copy in inputs[0] + inputs[1] + [whole]:
         copy.start()
     stores = []
 
@@ -481,8 +497,8 @@
 
     rows = GY * FZ
     for core in range(2):
-        inputs[core].wait()
         for slot in range(SLAB):
+            inputs[core][slot].wait()
             f_out[pl.ds(core * rows * SLAB + ORDER[slot], rows, stride=SLAB), :] = f_in[
                 core, pl.ds(FIELD_BASE[slot], rows), :
             ].astype(F32)
@@ -543,13 +559,13 @@
             pltpu.VMEM((SLAB, DROWS, LANES), BF),
             pltpu.VMEM((SLAB, DROWS, LANES), BF),
             pltpu.VMEM((DROWS + 16, LANES), F32),
-            pltpu.VMEM((AF_PIECES, 7, AF_ROWS // 8, LANES), BF),
+            pltpu.VMEM((7 * AF_TOTAL // 8, LANES), BF),
             pltpu.VMEM((2, W_SLOT, LANES), BF),
             pltpu.VMEM((2, 3, W_PART, LANES), BF),
             pltpu.VMEM((2, W_PART, LANES), BF),
             dma((4,)), dma((10,)), dma((10,)),
-            dma((4,)), dma((4,)), dma((2, 7)), dma((2, 7)), dma((2, 7)), dma((2, 7)),
-            dma((2, 3)), dma((2, 3)), dma((2,)), dma((2,)), dma((2, 3)), dma((2, 3)), dma((4,)),
+            dma((5,)), dma((5,)), dma((3, 7)), dma((3, 7)), dma((3, 7)), dma((3, 7)),
+            dma((2, 3)), dma((2, 3)), dma((2,)), dma((2,)), dma((2, 3)), dma((2, 3)), dma((5,)),
         ],
         compiler_params=pltpu.CompilerParams(
             collective_id=0, has_side_effects=True, vmem_limit_bytes=56 * 1024 * 1024
@@ -571,7 +587,7 @@
             pltpu.VMEM((2 * W_SLOT, LANES), BF),
             pltpu.VMEM((SLAB * FY * FZ, LANES), F32),
             pltpu.VMEM((2 * GRAD, LANES), F32),
-            dma((3,)), dma((12,)),
+            dma((3, SLAB)), dma((12,)),
         ],
         compiler_params=pltpu.CompilerParams(vmem_limit_bytes=56 * 1024 * 1024),
         cost_estimate=pl.CostEstimate(flops=0, bytes_accessed=5_000_000, transcendentals=0),

time: 45.3 us -> 45.6 us (level)
  no operation moved by 1% of the time
where the time goes in v5:
time: 45.6 us; the launch traced here: 45.4 us
  Pallas kernels  44.8 us (98%)
  between operations  0.64 us (1%)
    pallas_call x1, Pallas kernels, shards(): pl.pallas_call(kernel, out_shape=(jax.ShapeDtypeStruct((2, AF_TOTAL, LANE...  41.9 us
    pallas_call x1, Pallas kernels, shards(): pl.pallas_call(finish, out_shape=(jax.ShapeDtypeStruct((SLAB * CY * CZ, L...  2.95 us

profile of v5, /device:TPU:1, one launch (start us, length us, event | category | flops | bytes accessed | tf_op | source)
XLA Modules:
  0.0 45.4 jit_solution(6445453376586913410)
XLA Ops:
  0.6 41.9 %shard_map.75 = (bf16[2,2560,128]{2,1,0:T(8,128)(2,1)}, bf16[1792,128]{1,0:T(8,128)(2,1)}) custom-call(bf16[2880,128]{1,0:T(8,128)(2,1)} %bitcast.16, bf16[4,16,32,128]{3,2,1,0:T(8,128)(2,1)} %cot.1, bf16[864,128]{1,0:T(8,128)(2,1)} %bitcast.20, bf16[864,128]{1,0:T(8,128)(2,1)} %bitcast.21), custom_call_target="tpu_custom_call" | custom-call | flops 4000000000 | bytes 8000000 | tf_op jit(solution)/shard_map/pallas_call | solution.py:527
  42.5 2.9 %shard_map.76 = (bf16[2048,128]{1,0:T(8,128)(2,1)}, f32[2880,128]{1,0:T(8,128)}, f32[864,128]{1,0:T(8,128)}, f32[864,128]{1,0:T(8,128)}) custom-call(bf16[2,2560,128]{2,1,0:T(8,128)(2,1)} %get-tuple-element.10.full, bf16[1792,128]{1,0:T(8,128)(2,1)} %get-tuple-element.11.grads), custom_call_target="tpu_custom_call" | custom-call | bytes 5000000 | tf_op jit(solution)/shard_map/pallas_call | solution.py:575

commit v6 on v5

--- a/solution.py
+++ b/solution.py
@@ -287,14 +287,11 @@
         arrived(k)
         stage_one(x)
 
-    sends = []
-
     def send(src, dst, send_sem, recv_sem, peer):
         copy = pltpu.make_async_remote_copy(
             src_ref=src, dst_ref=dst, send_sem=send_sem, recv_sem=recv_sem, device_id=peer, device_id_type=MESH
         )
         copy.start()
-        sends.append(copy)
         return copy
 
     def scatter(peers, piece, landing, size, sems):
@@ -320,12 +317,23 @@
         store.start()
         stores.append(store)
 
-    class AfSum:
+    class Sum:
+        def __init__(self):
+            self.step, self.copies, self.before = 0, [], []
+
+        def advance(self):
+            for copy in self.before:
+                copy.wait_send()
+            self.before = self.copies
+            self.take()
+            self.step += 1
+
+    class AfSum(Sum):
         def __init__(self, p):
             self.p, self.rows, self.size, self.base = p, AF_ROWS[p], AF_ROWS[p] // 8, AF_BASE[p]
             self.me = xl * 4 + y
             self.landing = lambda j: land_af.at[pl.ds(AF_LAND[p] + j * self.size, self.size)]
-            self.step = 0
+            super().__init__()
 
         def piece(self, off, size):
             return B.at[pl.ds(align(self.base + off), size)]
@@ -333,7 +341,7 @@
         def whole(self, off, size):
             return R.at[pl.ds(align(self.base + off), size)]
 
-        def advance(self):
+        def take(self):
             p, me, size = self.p, self.me, self.size
             if self.step == 0:
                 sems = (lambda j: rs_s.at[p, j], lambda j: rs_r.at[p, j])
@@ -353,18 +361,17 @@
                 keep(rows, there, p)
             else:
                 self.copies[0].wait_recv()
-            self.step += 1
-
-    class GxSum:
+
+    class GxSum(Sum):
         def __init__(self, p):
             self.p, self.base = p, p * W_SLOT
             self.landing = lambda j: land_z.at[p, j]
-            self.step = 0
+            super().__init__()
 
         def piece(self, off, size):
             return WB.at[core, pl.ds(align(self.base + off), size)]
 
-        def advance(self):
+        def take(self):
             p, rows = self.p, pl.ds(self.base, W_SLOT)
             if self.step == 0:
                 self.copies = [
@@ -391,7 +398,6 @@
             else:
                 for copy in self.copies:
                     copy.wait_recv()
-            self.step += 1
 
     stores = []
     inner_planes, low_plane, high_plane = AfSum(0), AfSum(1), AfSum(2)
@@ -452,6 +458,8 @@
     out_plane(3)
     field_plane(3)
     high_plane.advance()
+    for copy in halos:
+        copy.wait_send()
     inner_planes.advance()
     outer_sum.advance()
     inner_sum.advance()
@@ -469,24 +477,15 @@
     inner_sum.advance()
     for store in stores:
         store.wait()
-    for copy in halos + sends:
-        copy.wait_send()
+    for item in (inner_planes, low_plane, high_plane, inner_sum, outer_sum):
+        for copy in item.before:
+            copy.wait_send()
 
 
 def finish(full, grads, out_ref, field_ref, inner_ref, outer_ref, f_in, g_in, f_out, w_out, in_sem, out_sem):
-    inputs = [
-        [
-            pltpu.make_async_copy(
-                full.at[core, pl.ds(slot * PLANE_ROWS, PLANE_ROWS)],
-                f_in.at[core, pl.ds(slot * PLANE_ROWS, PLANE_ROWS)],
-                in_sem.at[core, slot],
-            )
-            for slot in range(SLAB)
-        ]
-        for core in range(2)
-    ]
-    whole = pltpu.make_async_copy(grads, g_in, in_sem.at[2, 0])
-    for copy in inputs[0] + inputs[1] + [whole]:
+    inputs = [pltpu.make_async_copy(full.at[core], f_in.at[core], in_sem.at[core]) for core in range(2)]
+    whole = pltpu.make_async_copy(grads, g_in, in_sem.at[2])
+    for copy in inputs + [whole]:
         copy.start()
     stores = []
 
@@ -497,8 +496,8 @@
 
     rows = GY * FZ
     for core in range(2):
+        inputs[core].wait()
         for slot in range(SLAB):
-            inputs[core][slot].wait()
             f_out[pl.ds(core * rows * SLAB + ORDER[slot], rows, stride=SLAB), :] = f_in[
                 core, pl.ds(FIELD_BASE[slot], rows), :
             ].astype(F32)
@@ -587,7 +586,7 @@
             pltpu.VMEM((2 * W_SLOT, LANES), BF),
             pltpu.VMEM((SLAB * FY * FZ, LANES), F32),
             pltpu.VMEM((2 * GRAD, LANES), F32),
-            dma((3, SLAB)), dma((12,)),
+            dma((3,)), dma((12,)),
         ],
         compiler_params=pltpu.CompilerParams(vmem_limit_bytes=56 * 1024 * 1024),
         cost_estimate=pl.CostEstimate(flops=0, bytes_accessed=5_000_000, transcendentals=0),

time: 45.6 us -> 45.4 us (level)
  no operation moved by 1% of the time
where the time goes in v6:
time: 45.4 us; the launch traced here: 45.3 us
  Pallas kernels  44.6 us (98%)
  between operations  0.64 us (1%)
    pallas_call x1, Pallas kernels, shards(): pl.pallas_call(kernel, out_shape=(jax.ShapeDtypeStruct((2, AF_TOTAL, LANE...  41.8 us
    pallas_call x1, Pallas kernels, shards(): pl.pallas_call(finish, out_shape=(jax.ShapeDtypeStruct((SLAB * CY * CZ, L...  2.87 us

profile of v6, /device:TPU:1, one launch (start us, length us, event | category | flops | bytes accessed | tf_op | source)
XLA Modules:
  0.0 45.3 jit_solution(3527459772689219869)
XLA Ops:
  0.6 41.8 %shard_map.75 = (bf16[2,2560,128]{2,1,0:T(8,128)(2,1)}, bf16[1792,128]{1,0:T(8,128)(2,1)}) custom-call(bf16[2880,128]{1,0:T(8,128)(2,1)} %bitcast.16, bf16[4,16,32,128]{3,2,1,0:T(8,128)(2,1)} %cot.1, bf16[864,128]{1,0:T(8,128)(2,1)} %bitcast.20, bf16[864,128]{1,0:T(8,128)(2,1)} %bitcast.21), custom_call_target="tpu_custom_call" | custom-call | flops 4000000000 | bytes 8000000 | tf_op jit(solution)/shard_map/pallas_call | solution.py:526
  42.4 2.9 %shard_map.76 = (bf16[2048,128]{1,0:T(8,128)(2,1)}, f32[2880,128]{1,0:T(8,128)}, f32[864,128]{1,0:T(8,128)}, f32[864,128]{1,0:T(8,128)}) custom-call(bf16[2,2560,128]{2,1,0:T(8,128)(2,1)} %get-tuple-element.10.full, bf16[1792,128]{1,0:T(8,128)(2,1)} %get-tuple-element.11.grads), custom_call_target="tpu_custom_call" | custom-call | bytes 5000000 | tf_op jit(solution)/shard_map/pallas_call | solution.py:574

commit v7 on v4

--- a/solution.py
+++ b/solution.py
@@ -434,13 +434,13 @@
 
     edge_outer()
     outer_sum.advance()
-    edge_inner()
-    inner_sum.advance()
     out_plane(0)
     out_plane(1)
     field_plane(0)
     field_plane(1)
     inner_planes.advance()
+    edge_inner()
+    inner_sum.advance()
     far_planes()
     outer_sum.advance()
     inner_sum.advance()

time: 45.3 us -> 46.1 us (1.018)
  Pallas kernels: 44.5 us -> 45.3 us
    pallas_call x1, Pallas kernels: 41.6 us -> 42.4 us  [shards(): pl.pallas_call(kernel, out_shape=(jax.ShapeDtypeStruct((2, AF_TOTAL, LANE...]
where the time goes in v7:
time: 46.1 us; the launch traced here: 46 us
  Pallas kernels  45.3 us (98%)
  between operations  0.64 us (1%)
    pallas_call x1, Pallas kernels, shards(): pl.pallas_call(kernel, out_shape=(jax.ShapeDtypeStruct((2, AF_TOTAL, LANE...  42.4 us
    pallas_call x1, Pallas kernels, shards(): pl.pallas_call(finish, out_shape=(jax.ShapeDtypeStruct((SLAB * CY * CZ, L...  2.87 us

profile of v7, /device:TPU:1, one launch (start us, length us, event | category | flops | bytes accessed | tf_op | source)
XLA Modules:
  0.0 46.0 jit_solution(4821974278130165278)
XLA Ops:
  0.6 42.4 %shard_map.75 = (bf16[2,2560,128]{2,1,0:T(8,128)(2,1)}, bf16[1792,128]{1,0:T(8,128)(2,1)}) custom-call(bf16[2880,128]{1,0:T(8,128)(2,1)} %bitcast.16, bf16[4,16,32,128]{3,2,1,0:T(8,128)(2,1)} %cot.1, bf16[864,128]{1,0:T(8,128)(2,1)} %bitcast.20, bf16[864,128]{1,0:T(8,128)(2,1)} %bitcast.21), custom_call_target="tpu_custom_call" | custom-call | flops 4000000000 | bytes 8000000 | tf_op jit(solution)/shard_map/pallas_call | solution.py:511
  43.1 2.9 %shard_map.76 = (bf16[2048,128]{1,0:T(8,128)(2,1)}, f32[2880,128]{1,0:T(8,128)}, f32[864,128]{1,0:T(8,128)}, f32[864,128]{1,0:T(8,128)}) custom-call(bf16[2,2560,128]{2,1,0:T(8,128)(2,1)} %get-tuple-element.10.full, bf16[1792,128]{1,0:T(8,128)(2,1)} %get-tuple-element.11.grads), custom_call_target="tpu_custom_call" | custom-call | bytes 5000000 | tf_op jit(solution)/shard_map/pallas_call | solution.py:559
